TPU v7x, 128 devices: a whole 4x4x4 slice. The times are simulated.
128 devices in a mesh: lat: 8 (over z, core), lon: 16 (over x, y).
Axes of the slice: x: 4, y: 4, z: 4, core: 2. Of those that a mesh axis runs over, the one named last changes fastest.
Arguments:
- grid_in: bfloat16 [32768, 512], P(('lat', 'lon')), may hold values from -6 to 6
- mesh_in: bfloat16 [8192, 512], P(('lat', 'lon')), may hold values from -6 to 6
- encode_sources: int32 [73728], P(('lat', 'lon')), may hold values from 0 to 255
- encode_targets: int32 [73728], P(('lat', 'lon')), may hold values from -1 to 63, as said below
- encode_edges: float32 [4, 73728], P(None, ('lat', 'lon')), may hold values from -6 to 6
- border_rows: int32 [16, 32, 32], P('lat', 'lon'), may hold values from 0 to 63
- process_sources: int32 [131072], P(('lat', 'lon')), may hold values from 0 to 447, as said below
- process_targets: int32 [131072], P(('lat', 'lon')), may hold values from 0 to 63
- process_edges: float32 [4, 131072], P(None, ('lat', 'lon')), may hold values from -6 to 6
- decode_sources: int32 [110592], P(('lat', 'lon')), may hold values from 0 to 63
- decode_targets: int32 [110592], P(('lat', 'lon')), may hold values from -1 to 255, as said below
- decode_edges: float32 [4, 110592], P(None, ('lat', 'lon')), may hold values from -6 to 6
- refine_hidden: bfloat16 [512, 512], replicated, may hold values from -0.25 to 0.25
- refine_output: bfloat16 [512, 512], replicated, may hold values from -0.25 to 0.25
- encode_source: bfloat16 [512, 512], replicated, may hold values from -0.25 to 0.25
- encode_target: bfloat16 [512, 512], replicated, may hold values from -0.25 to 0.25
- encode_geometry: float32 [4, 512], replicated, may hold values from -3 to 3
- encode_output: bfloat16 [512, 512], replicated, may hold values from -0.25 to 0.25
- mesh_self: bfloat16 [512, 512], replicated, may hold values from -0.1875 to 0.1875
- mesh_gather: bfloat16 [512, 512], replicated, may hold values from -0.1875 to 0.1875
- mesh_output: bfloat16 [512, 512], replicated, may hold values from -0.25 to 0.25
- process_source: bfloat16 [512, 512], replicated, may hold values from -0.25 to 0.25
- process_target: bfloat16 [512, 512], replicated, may hold values from -0.25 to 0.25
- process_geometry: float32 [4, 512], replicated, may hold values from -3 to 3
- process_output: bfloat16 [512, 512], replicated, may hold values from -0.25 to 0.25
- node_self: bfloat16 [512, 512], replicated, may hold values from -0.1875 to 0.1875
- node_gather: bfloat16 [512, 512], replicated, may hold values from -0.1875 to 0.1875
- node_output: bfloat16 [512, 512], replicated, may hold values from -0.25 to 0.25
- decode_source: bfloat16 [512, 512], replicated, may hold values from -0.25 to 0.25
- decode_target: bfloat16 [512, 512], replicated, may hold values from -0.25 to 0.25
- decode_geometry: float32 [4, 512], replicated, may hold values from -3 to 3
- decode_output: bfloat16 [512, 512], replicated, may hold values from -0.25 to 0.25
- grid_self: bfloat16 [512, 512], replicated, may hold values from -0.1875 to 0.1875
- grid_gather: bfloat16 [512, 512], replicated, may hold values from -0.1875 to 0.1875
- grid_output: bfloat16 [512, 512], replicated, may hold values from -0.25 to 0.25
Outputs:
- grid_out: bfloat16 [32768, 512], P(('lat', 'lon'))
- mesh_out: bfloat16 [8192, 512], P(('lat', 'lon'))
Inputs may be any that keep to these rules, and one draw needn't show every extreme that they name: `encode_targets`: in each receiving partition the slots come in nine groups of 64, one per sending neighbour; the filled slots of a group come first and hold mesh rows; groups whose sender would lie past a pole are empty; in each receiving partition one group from its own band is complete. `decode_targets`: in each receiving partition the slots come in nine groups of 96, one per sending neighbour; the filled slots of a group come first and hold grid rows; groups whose sender would lie past a pole are empty; in each receiving partition one group from its own band is complete. `process_sources`: in each partition the first half of the edges have senders below 64, the second half at or above it.
All inputs are finite; a program needn't handle non-finite values.
Results may differ from a plain program's by a relative error of at most 0.012.
Values may be sent and summed in bfloat16 or wider, within the bound.
A program may use at most 64 MiB of HBM per device.

v0:
```python
import jax
import jax.numpy as jnp
from jax import lax
from jax.sharding import PartitionSpec as P


def with_halo(cells, sides, width):
    for axis, dim in sides:
        count = lax.axis_size(axis)
        head = lax.slice_in_dim(cells, 0, width, axis=dim)
        tail = lax.slice_in_dim(cells, cells.shape[dim] - width, cells.shape[dim], axis=dim)
        cells = jnp.concatenate(
            [
                lax.ppermute(tail, axis, [(i, (i + 1) % count) for i in range(count)]),
                cells,
                lax.ppermute(head, axis, [((i + 1) % count, i) for i in range(count)]),
            ],
            axis=dim,
        )
    return cells


def layer_norm(values):
    average = jnp.mean(values, axis=-1, keepdims=True)
    centred = values - average
    variance = jnp.mean(centred * centred, axis=-1, keepdims=True)
    return centred * lax.rsqrt(variance + 1e-05)


def project(operand, weights):
    return jnp.dot(operand, weights, preferred_element_type=jnp.float32)


def geometry_term(edges, weights):
    return jnp.einsum("gs,gd->sd", edges, weights, precision=lax.Precision.HIGHEST)


def edge_sum(activation, targets, target_term, output_weights, segments):
    filled = targets >= 0
    safe_rows = jnp.where(filled, targets, 0)
    hidden = jax.nn.silu(
        activation.astype(jnp.float32) + jnp.take(target_term, safe_rows, axis=0)
    ).astype(jnp.bfloat16)
    message = layer_norm(project(hidden, output_weights))
    segment_ids = jnp.where(filled, targets, segments)
    return jax.ops.segment_sum(message, segment_ids, num_segments=segments + 1)[:segments]


def process_sum(activation, targets, output_weights, segments):
    hidden = jax.nn.silu(activation).astype(jnp.bfloat16)
    message = layer_norm(project(hidden, output_weights))
    return jax.ops.segment_sum(message, targets, num_segments=segments)


def node_update(state, gathered, self_weights, gather_weights, output_weights):
    hidden = jax.nn.silu(project(state, self_weights) + project(gathered, gather_weights)).astype(
        jnp.bfloat16
    )
    return (state.astype(jnp.float32) + layer_norm(project(hidden, output_weights))).astype(
        jnp.bfloat16
    )


def refine(grid_rows, hidden_weights, output_weights):
    hidden = jax.nn.silu(project(grid_rows, hidden_weights)).astype(jnp.bfloat16)
    return (grid_rows.astype(jnp.float32) + layer_norm(project(hidden, output_weights))).astype(
        jnp.bfloat16
    )


def gather_cycle(payload):
    features = payload.shape[-1]
    window = with_halo(payload, (("lat", 0), ("lon", 1)), 1)
    band = lax.axis_index("lat")
    lower_rim = jnp.where(band > 0, window[0], jnp.zeros_like(window[0]))
    upper_rim = jnp.where(band < lax.axis_size("lat") - 1, window[3], jnp.zeros_like(window[3]))
    return jnp.concatenate(
        [
            lower_rim.reshape(-1, features),
            window[1, 0],
            window[1, 3],
            window[2, 0],
            window[2, 3],
            upper_rim.reshape(-1, features),
        ],
        axis=0,
    )


def body(
    grid_in,
    mesh_in,
    encode_sources,
    encode_targets,
    encode_edges,
    border_rows,
    process_sources,
    process_targets,
    process_edges,
    decode_sources,
    decode_targets,
    decode_edges,
    refine_hidden,
    refine_output,
    encode_source,
    encode_target,
    encode_geometry,
    encode_output,
    mesh_self,
    mesh_gather,
    mesh_output,
    process_source,
    process_target,
    process_geometry,
    process_output,
    node_self,
    node_gather,
    node_output,
    decode_source,
    decode_target,
    decode_geometry,
    decode_output,
    grid_self,
    grid_gather,
    grid_output,
):
    features = grid_in.shape[1]
    grid_count = grid_in.shape[0]
    mesh_count = mesh_in.shape[0]
    refined = refine(grid_in, refine_hidden, refine_output)
    source_term = project(grid_in, encode_source)
    outgoing = (
        jnp.take(source_term, encode_sources, axis=0) + geometry_term(encode_edges, encode_geometry)
    ).astype(jnp.bfloat16)
    grouped = outgoing.reshape(3, 3, -1, features)
    window = with_halo(grouped, (("lat", 0), ("lon", 1)), 1)
    arrived = window[4::-2, 4::-2].reshape(-1, features)
    encode_total = edge_sum(
        arrived, encode_targets, project(mesh_in, encode_target), encode_output, mesh_count
    )
    mesh_one = node_update(
        mesh_in, encode_total.astype(jnp.bfloat16), mesh_self, mesh_gather, mesh_output
    )
    payload = jnp.take(mesh_one, border_rows.reshape(-1), axis=0).reshape(2, 2, -1, features)
    local_source = project(mesh_one, process_source)
    local_target = project(mesh_one, process_target)
    geometry = geometry_term(process_edges, process_geometry)
    source_table = jnp.concatenate(
        [local_source, project(gather_cycle(payload), process_source)], axis=0
    )
    activation = (
        jnp.take(source_table, process_sources, axis=0)
        + jnp.take(local_target, process_targets, axis=0)
        + geometry
    )
    process_total = process_sum(activation, process_targets, process_output, mesh_count)
    mesh_out = node_update(
        mesh_one, process_total.astype(jnp.bfloat16), node_self, node_gather, node_output
    )
    leaving = (
        jnp.take(project(mesh_out, decode_source), decode_sources, axis=0)
        + geometry_term(decode_edges, decode_geometry)
    ).astype(jnp.bfloat16)
    grouped_back = leaving.reshape(3, 3, -1, features)
    window_back = with_halo(grouped_back, (("lat", 0), ("lon", 1)), 1)
    returned = window_back[4::-2, 4::-2].reshape(-1, features)
    decode_total = edge_sum(
        returned, decode_targets, project(refined, decode_target), decode_output, grid_count
    )
    grid_out = node_update(
        refined, decode_total.astype(jnp.bfloat16), grid_self, grid_gather, grid_output
    )
    return (grid_out, mesh_out)


def solution(mesh):
    placed = (
        P(("lat", "lon"), None),
        P(("lat", "lon"), None),
        P(("lat", "lon")),
        P(("lat", "lon")),
        P(None, ("lat", "lon")),
        P("lat", "lon", None),
        P(("lat", "lon")),
        P(("lat", "lon")),
        P(None, ("lat", "lon")),
        P(("lat", "lon")),
        P(("lat", "lon")),
        P(None, ("lat", "lon")),
        P(),
        P(),
        P(),
        P(),
        P(),
        P(),
        P(),
        P(),
        P(),
        P(),
        P(),
        P(),
        P(),
        P(),
        P(),
        P(),
        P(),
        P(),
        P(),
        P(),
        P(),
        P(),
        P(),
    )
    return jax.shard_map(
        body,
        mesh=mesh,
        in_specs=placed,
        out_specs=(P(("lat", "lon"), None), P(("lat", "lon"), None)),
        check_vma=False,
    )
```

profile of v0, /device:TPU:1, one launch (start us, length us, event | category | flops | bytes accessed | tf_op | source)
XLA Modules:
  0.0 135.0 jit_solution(10710096197901516734)
XLA Ops:
  0.6 0.7 compare_select_fusion.8
  1.4 0.7 compare_and_fusion.5
  2.1 0.7 pad_clamp_fusion.4
  2.8 1.4 %fusion.54 = f32[256,512]{1,0:T(8,128)S(1)} fusion(bf16[256,512]{1,0:T(8,128)(2,1)} %param.35, bf16[512,512]{1,0:T(8,128)(2,1)} %param.49), kind=kOutput, calls=%fused_computation.151 | convolution fusion | flops 134217728 | bytes 1310720 | tf_op jit(solution)/shard_map/dot_general | solution.py:31
  4.2 2.2 %gather_fusion = f32[576,512]{1,0:T(8,128)S(1)} fusion(f32[256,512]{1,0:T(8,128)S(1)} %fusion.54, s32[1024]{0:T(1024)S(1)} %get-tuple-element.36), kind=kCustom, calls=%fused_computation | custom fusion | bytes 2361600 | tf_op jit(solution)/shard_map/jit(_take)/gather | solution.py:133
  6.5 1.2 fusion.3
  7.7 0.8 fusion.38
  8.5 3.0 %collective-permute-start = (bf16[1,3,64,512]{3,2,1,0:T(8,128)(2,1)}, bf16[1,3,64,512]{3,2,1,0:T(8,128)(2,1)S(1)}, u32[]{:S(2)}, u32[]{:S(2)}) collective-permute-start(bf16[1,3,64,512]{3,2,1,0:T(8,128)(2,1)} %bitcast), channel_id=1, source_target_pairs={{0,16},{16,32},{32,48},{48,64},{64,80},{80,96},{96,112},{112,0},{1... | collective-permute-start | bytes 589832 | tf_op jit(solution)/shard_map/ppermute | solution.py:14
  14.9 1.9 %fusion.53 = f32[64,512]{1,0:T(8,128)} fusion(bf16[64,512]{1,0:T(8,128)(2,1)S(1)} %copy-done.4, bf16[512,512]{1,0:T(8,128)(2,1)} %param.53), kind=kOutput, calls=%fused_computation.150 | convolution fusion | flops 33554432 | bytes 720896 | tf_op jit(solution)/shard_map/dot_general | solution.py:31
  16.8 0.7 fusion.41
  18.2 2.2 %gather_fusion.1 = f32[576,512]{1,0:T(8,128)S(1)} fusion(f32[64,512]{1,0:T(8,128)S(1)} %fusion.55, s32[1024]{0:T(1024)S(1)} %pad_clamp_fusion.3), kind=kCustom, calls=%fused_computation.1 | custom fusion | bytes 2361600 | tf_op jit(solution)/shard_map/jit(_take)/gather | solution.py:42
  21.0 1.0 pad_maximum_fusion.8
  22.0 1.4 %collective-permute-start.2 = (bf16[5,1,64,512]{3,2,1,0:T(8,128)(2,1)S(1)}, bf16[5,1,64,512]{3,2,1,0:T(8,128)(2,1)S(1)}, u32[]{:S(2)}, u32[]{:S(2)}) collective-permute-start(bf16[5,1,64,512]{3,2,1,0:T(8,128)(2,1)S(1)} %get-tuple-element.4), channel_id=1, source_target_pairs={{0,1},{1,2},{2,3},{3,4},{4,5},{5,6},{6,7},{7,8},{8,9},{9,10},{10,1... | collective-permute-start | bytes 983048 | tf_op jit(solution)/shard_map/ppermute | solution.py:14
  23.3 3.7 %collective-permute-start.3 = (bf16[5,1,64,512]{3,2,1,0:T(8,128)(2,1)S(1)}, bf16[5,1,64,512]{3,2,1,0:T(8,128)(2,1)S(1)}, u32[]{:S(2)}, u32[]{:S(2)}) collective-permute-start(bf16[5,1,64,512]{3,2,1,0:T(8,128)(2,1)S(1)} %get-tuple-element.5), channel_id=1, source_target_pairs={{1,0},{2,1},{3,2},{4,3},{5,4},{6,5},{7,6},{8,7},{9,8},{10,9},{11,1... | collective-permute-start | bytes 983048 | tf_op jit(solution)/shard_map/ppermute | solution.py:16
  27.6 0.8 add_convert_fusion.2
  28.5 4.4 %collective-permute-done.2 = bf16[5,1,64,512]{3,2,1,0:T(8,128)(2,1)S(1)} collective-permute-done((bf16[5,1,64,512]{3,2,1,0:T(8,128)(2,1)S(1)}, bf16[5,1,64,512]{3,2,1,0:T(8,128)(2,1)S(1)}, u32[]{:S(2)}, u32[]{:S(2)}) %collective-permute-start.2) | collective-permute-done | bytes 327712 | tf_op jit(solution)/shard_map/ppermute | solution.py:14
  32.9 1.2 pad_maximum_fusion.1
  36.7 7.7 %scatter_custom_fusion = f32[65,512]{1,0:T(8,128)S(1)} fusion(s32[576]{0:T(1024)} %get-tuple-element.17, f32[576,512]{1,0:T(8,128)S(1)} %get-tuple-element.23, f32[576]{0:T(1024)S(1)} %add_rsqrt_fusion.2, f32[576]{0:T(1024)S(1)} %broadcast_multiply_fusion.2, f32[]{:T(128)} %constant.106.clone.1), kind=kCustom, calls=%fused_computation.26 | custom fusion | flops 884736 | bytes 1317888 | tf_op jit(solution)/shard_map/scatter-add | solution.py:46
  45.3 1.0 gather_fusion.2
  46.4 4.3 %collective-permute-start.4 = (bf16[1,2,32,512]{3,2,1,0:T(8,128)(2,1)S(1)}, bf16[1,2,32,512]{3,2,1,0:T(8,128)(2,1)S(1)}, u32[]{:S(2)}, u32[]{:S(2)}) collective-permute-start(bf16[1,2,32,512]{3,2,1,0:T(8,128)(2,1)S(1)} %bitcast.86), channel_id=1, source_target_pairs={{0,16},{16,32},{32,48},{48,64},{64,80},{80,96},{96,112},{112,0},{1... | collective-permute-start | bytes 196616 | tf_op jit(solution)/shard_map/ppermute | solution.py:14
  51.2 4.8 %gather_fusion.4 = f32[1024,512]{1,0:T(8,128)} fusion(f32[64,512]{1,0:T(8,128)S(1)} %fusion.59, s32[1024]{0:T(1024)S(1)} %fusion.31), kind=kCustom, calls=%fused_computation.4 | custom fusion | bytes 4198400 | tf_op jit(solution)/shard_map/jit(_take)/gather | solution.py:153
  56.1 5.1 %collective-permute-start.7 = (bf16[4,1,32,512]{3,2,1,0:T(8,128)(2,1)S(1)}, bf16[4,1,32,512]{3,2,1,0:T(8,128)(2,1)S(1)}, u32[]{:S(2)}, u32[]{:S(2)}) collective-permute-start(bf16[4,1,32,512]{3,2,1,0:T(8,128)(2,1)S(1)} %get-tuple-element.13), channel_id=1, source_target_pairs={{1,0},{2,1},{3,2},{4,3},{5,4},{6,5},{7,6},{8,7},{9,8},{10,9},{11,1... | collective-permute-start | bytes 393224 | tf_op jit(solution)/shard_map/ppermute | solution.py:16
  61.2 0.9 fusion.56
  62.1 1.2 collective-permute-done.6
  64.0 4.9 %gather_fusion.3 = f32[1024,512]{1,0:T(8,128)} fusion(f32[448,512]{1,0:T(8,128)S(1)} %pad_maximum_fusion.2, s32[1024]{0:T(1024)S(1)} %get-tuple-element.37), kind=kCustom, calls=%fused_computation.3 | custom fusion | bytes 4198400 | tf_op jit(solution)/shard_map/jit(_take)/gather | solution.py:152
  68.9 4.4 %multiply_convert_fusion = bf16[1024,512]{1,0:T(8,128)(2,1)S(1)} fusion(f32[1024,512]{1,0:T(8,128)} %gather_fusion.4, f32[1024,512]{1,0:T(8,128)} %gather_fusion.3, f32[4,1024]{1,0:T(4,128)S(1)} %copy-done.38, f32[4,512]{1,0:T(4,128)S(1)} %copy-done.39, pred[1024]{0:T(1024)(128)(4,1)S(1)} %copy-done.33, pred[1024]{0:T(1024)(128)(4,1)S(1)} %copy-done.34), kind=kOutput, calls=%fused_computation.12 | convolution fusion | flops 29884416 | bytes 5269504 | tf_op jit(solution)/shard_map/gs,gd->sd/dot_general | solution.py:35
  73.3 0.8 fusion.44
  74.7 1.8 %copy.37 = f32[1024,512]{1,0:T(8,128)} copy(f32[1024,512]{0,1:T(8,128)S(1)} %subtract_multiply_fusion) | data formatting | bytes 4194304 | tf_op jit(solution)/shard_map/mul | solution.py:27
  76.6 7.3 %scatter_custom_fusion.1 = f32[64,512]{1,0:T(8,128)S(1)} fusion(s32[1024]{0:T(1024)S(1)} %copy-done.23, f32[1024,512]{1,0:T(8,128)} %copy.37, f32[]{:T(128)} %constant.106.clone.1), kind=kCustom, calls=%fused_computation.76 | custom fusion | flops 524288 | bytes 131584 | tf_op jit(solution)/shard_map/scatter-add | solution.py:52
  83.9 1.6 %fusion.45 = (f32[64]{0:T(128)S(1)}, f32[64,512]{1,0:T(8,128)S(1)}) fusion(bf16[512,512]{1,0:T(8,128)(2,1)S(1)} %copy-done.12, f32[64,512]{1,0:T(8,128)} %fusion.56, bf16[512,512]{1,0:T(8,128)(2,1)} %param.61, f32[64,512]{1,0:T(8,128)S(1)} %scatter_custom_fusion.1), kind=kOutput, calls=%fused_computation.145 | convolution fusion | flops 67370944 | bytes 1442048 | tf_op jit(solution)/shard_map/dot_general | solution.py:31
  86.1 2.8 %gather_fusion.5 = f32[864,512]{1,0:T(8,128)S(1)} fusion(f32[64,512]{1,0:T(8,128)S(1)} %fusion.60, s32[1024]{0:T(1024)S(1)} %get-tuple-element.34), kind=kCustom, calls=%fused_computation.5 | custom fusion | bytes 3542400 | tf_op jit(solution)/shard_map/jit(_take)/gather | solution.py:161
  88.9 1.7 %add_convert_fusion = bf16[864,512]{1,0:T(8,128)(2,1)S(1)} fusion(f32[864,512]{1,0:T(8,128)S(1)} %gather_fusion.5, f32[4,864]{1,0:T(4,128)S(1)} %copy-done.25, f32[4,512]{1,0:T(4,128)S(1)} %copy-done.29, pred[864]{0:T(1024)(128)(4,1)S(1)} %copy-done.30), kind=kOutput, calls=%fused_computation.19 | convolution fusion | flops 22560768 | bytes 2677088 | tf_op jit(solution)/shard_map/gs,gd->sd/dot_general | solution.py:35
  90.7 3.4 %collective-permute-start.8 = (bf16[1,3,96,512]{3,2,1,0:T(8,128)(2,1)S(1)}, bf16[1,3,96,512]{3,2,1,0:T(8,128)(2,1)S(1)}, u32[]{:S(2)}, u32[]{:S(2)}) collective-permute-start(bf16[1,3,96,512]{3,2,1,0:T(8,128)(2,1)S(1)} %bitcast.84), channel_id=1, source_target_pairs={{0,16},{16,32},{32,48},{48,64},{64,80},{80,96},{96,112},{112,0},{1... | collective-permute-start | bytes 884744 | tf_op jit(solution)/shard_map/ppermute | solution.py:14
  94.4 3.3 %collective-permute-done.8 = bf16[1,3,96,512]{3,2,1,0:T(8,128)(2,1)S(1)} collective-permute-done((bf16[1,3,96,512]{3,2,1,0:T(8,128)(2,1)S(1)}, bf16[1,3,96,512]{3,2,1,0:T(8,128)(2,1)S(1)}, u32[]{:S(2)}, u32[]{:S(2)}) %collective-permute-start.8) | collective-permute-done | bytes 294944 | tf_op jit(solution)/shard_map/ppermute | solution.py:14
  97.7 2.6 %collective-permute-done.9 = bf16[1,3,96,512]{3,2,1,0:T(8,128)(2,1)S(1)} collective-permute-done((bf16[1,3,96,512]{3,2,1,0:T(8,128)(2,1)S(1)}, bf16[1,3,96,512]{3,2,1,0:T(8,128)(2,1)S(1)}, u32[]{:S(2)}, u32[]{:S(2)}) %collective-permute-start.9) | collective-permute-done | bytes 294944 | tf_op jit(solution)/shard_map/ppermute | solution.py:16
  100.3 1.1 pad_maximum_fusion.5
  101.4 5.1 %collective-permute-start.11 = (bf16[5,1,96,512]{3,2,1,0:T(8,128)(2,1)}, bf16[5,1,96,512]{3,2,1,0:T(8,128)(2,1)}, u32[]{:S(2)}, u32[]{:S(2)}) collective-permute-start(bf16[5,1,96,512]{3,2,1,0:T(8,128)(2,1)} %get-tuple-element.3), channel_id=1, source_target_pairs={{1,0},{2,1},{3,2},{4,3},{5,4},{6,5},{7,6},{8,7},{9,8},{10,9},{11,1... | collective-permute-start | bytes 1474568 | tf_op jit(solution)/shard_map/ppermute | solution.py:16
  106.5 3.5 %gather_fusion.6 = f32[864,512]{1,0:T(8,128)} fusion(f32[256,512]{1,0:T(8,128)S(1)} %fusion.61, s32[1024]{0:T(1024)S(1)} %pad_clamp_fusion), kind=kCustom, calls=%fused_computation.6 | custom fusion | bytes 3542400 | tf_op jit(solution)/shard_map/jit(_take)/gather | solution.py:42
  110.1 1.1 fusion.52
  111.2 6.9 %collective-permute-done.10 = bf16[5,1,96,512]{3,2,1,0:T(8,128)(2,1)} collective-permute-done((bf16[5,1,96,512]{3,2,1,0:T(8,128)(2,1)}, bf16[5,1,96,512]{3,2,1,0:T(8,128)(2,1)}, u32[]{:S(2)}, u32[]{:S(2)}) %collective-permute-start.10) | collective-permute-done | bytes 491552 | tf_op jit(solution)/shard_map/ppermute | solution.py:14
  118.1 1.5 %pad_maximum_fusion = bf16[5,5,96,512]{3,2,1,0:T(8,128)(2,1)S(1)} fusion(bf16[5,1,96,512]{3,2,1,0:T(8,128)(2,1)} %collective-permute-done.11, bf16[1,3,96,512]{3,2,1,0:T(8,128)(2,1)S(1)} %collective-permute-done.9, bf16[3,3,96,512]{3,2,1,0:T(8,128)(2,1)S(1)} %bitcast.77, bf16[1,3,96,512]{3,2,1,0:T(8,128)(2,1)S(1)} %collective-permute-done.8, ...), kind=kLoop, calls=%fused_computation.10 | loop fusion | flops 4915200 | bytes 4915200 | tf_op jit(solution)/shard_map/concatenate | solution.py:12
  119.7 1.0 rev.7
  120.7 0.7 copy-done.1
  121.4 1.8 %multiply_convert_fusion.1 = bf16[864,512]{1,0:T(8,128)(2,1)S(1)} fusion(f32[864,512]{1,0:T(8,128)S(1)} %copy-done.1, bf16[3,3,96,512]{3,2,1,0:T(8,128)(2,1)} %rev.7, pred[864]{0:T(1024)(128)(4,1)S(1)} %compare_and_fusion), kind=kLoop, calls=%fused_computation.18 | loop fusion | flops 3538944 | bytes 3539808 | tf_op jit(solution)/shard_map/convert_element_type | solution.py:43
  123.3 0.7 fusion.48
  124.4 7.5 %scatter_custom_fusion.2 = f32[257,512]{1,0:T(8,128)S(1)} fusion(s32[864]{0:T(1024)S(1)} %get-tuple-element.19, f32[864,512]{1,0:T(8,128)S(1)} %get-tuple-element.31, f32[864]{0:T(1024)S(1)} %add_rsqrt_fusion, f32[864]{0:T(1024)S(1)} %broadcast_multiply_fusion, f32[]{:T(128)} %constant.106.clone.1), kind=kCustom, calls=%fused_computation.15 | custom fusion | flops 1327104 | bytes 2304004 | tf_op jit(solution)/shard_map/scatter-add | solution.py:46
  131.9 2.0 %fusion.49 = (f32[256]{0:T(256)S(1)}, f32[256,512]{1,0:T(8,128)S(1)}) fusion(bf16[512,512]{1,0:T(8,128)(2,1)} %param.69, f32[256,512]{1,0:T(8,128)} %fusion.52, bf16[512,512]{1,0:T(8,128)(2,1)} %param.68, f32[257,512]{1,0:T(8,128)S(1)} %scatter_custom_fusion.2), kind=kOutput, calls=%fused_computation.147 | convolution fusion | flops 269352704 | bytes 2360320 | tf_op jit(solution)/shard_map/dot_general | solution.py:31
  134.1 0.9 add_convert_fusion.1
  (157 shorter events, 12.2 us)
Async XLA Ops:
  0.6 72.6 %copy-start = (bf16[512,512]{1,0:T(8,128)(2,1)S(1)}, bf16[512,512]{1,0:T(8,128)(2,1)}, u32[]{:S(2)}) copy-start(bf16[512,512]{1,0:T(8,128)(2,1)} %param.59) | copy-start | bytes 1572868
  4.2 2.2 %copy-start.26 = (f32[4,576]{1,0:T(4,128)S(1)}, f32[4,576]{1,0:T(4,128)}, u32[]{:S(2)}) copy-start(f32[4,576]{1,0:T(4,128)} %param.39) | copy-start | bytes 27652
  4.2 2.2 %copy-start.28 = (f32[4,512]{1,0:T(4,128)S(1)}, f32[4,512]{1,0:T(4,128)}, u32[]{:S(2)}) copy-start(f32[4,512]{1,0:T(4,128)} %param.51) | copy-start | bytes 24580
  6.4 5.1 %copy-start.20 = (s32[576]{0:T(1024)S(1)}, s32[576]{0:T(1024)}, u32[]{:S(2)}) copy-start(s32[576]{0:T(1024)} %param.38) | copy-start | bytes 6916
  6.5 6.3 %copy-start.19 = (s32[2,2,32]{2,1,0:T(2,128)S(1)}, s32[2,2,32]{2,1,0:T(2,128)}, u32[]{:S(2)}) copy-start(s32[2,2,32]{2,1,0:T(2,128)} %param.40) | copy-start | bytes 1540
  6.5 7.0 %copy-start.23 = (s32[1024]{0:T(1024)S(1)}, s32[1024]{0:T(1024)}, u32[]{:S(2)}) copy-start(s32[1024]{0:T(1024)} %param.42) | copy-start | bytes 12292
  6.5 7.0 %copy-start.24 = (s32[1024]{0:T(1024)S(1)}, s32[1024]{0:T(1024)}, u32[]{:S(2)}) copy-start(s32[1024]{0:T(1024)} %param.41) | copy-start | bytes 12292
  6.5 7.5 %copy-start.22 = (s32[864]{0:T(1024)S(1)}, s32[864]{0:T(1024)}, u32[]{:S(2)}) copy-start(s32[864]{0:T(1024)} %param.44) | copy-start | bytes 10372
  6.5 8.1 %copy-start.4 = (bf16[64,512]{1,0:T(8,128)(2,1)S(1)}, bf16[64,512]{1,0:T(8,128)(2,1)}, u32[]{:S(2)}) copy-start(bf16[64,512]{1,0:T(8,128)(2,1)} %param.36) | copy-start | bytes 196612
  6.5 8.1 %copy-start.7 = (bf16[512,512]{1,0:T(8,128)(2,1)S(1)}, bf16[512,512]{1,0:T(8,128)(2,1)}, u32[]{:S(2)}) copy-start(bf16[512,512]{1,0:T(8,128)(2,1)} %param.50) | copy-start | bytes 1572868
  6.5 10.2 %copy-start.3 = (bf16[256,512]{1,0:T(8,128)(2,1)S(1)}, bf16[256,512]{1,0:T(8,128)(2,1)}, u32[]{:S(2)}) copy-start(bf16[256,512]{1,0:T(8,128)(2,1)} %param.35) | copy-start | bytes 786436
  7.7 9.1 %copy-start.36 = (bf16[512,512]{1,0:T(8,128)(2,1)S(1)}, bf16[512,512]{1,0:T(8,128)(2,1)}, u32[]{:S(2)}) copy-start(bf16[512,512]{1,0:T(8,128)(2,1)} %param.48) | copy-start | bytes 1572868
  7.7 9.0 %copy-start.37 = (bf16[512,512]{1,0:T(8,128)(2,1)S(1)}, bf16[512,512]{1,0:T(8,128)(2,1)}, u32[]{:S(2)}) copy-start(bf16[512,512]{1,0:T(8,128)(2,1)} %param.47) | copy-start | bytes 1572868
  8.5 12.5 %collective-permute-start = (bf16[1,3,64,512]{3,2,1,0:T(8,128)(2,1)}, bf16[1,3,64,512]{3,2,1,0:T(8,128)(2,1)S(1)}, u32[]{:S(2)}, u32[]{:S(2)}) collective-permute-start(bf16[1,3,64,512]{3,2,1,0:T(8,128)(2,1)} %bitcast), channel_id=1, source_target_pairs={{0,16},{16,32},{32,48},{48,64},{64,80},{80,96},{96,112},{112,0},{1... | collective-permute-start | bytes 589832 | tf_op jit(solution)/shard_map/ppermute | solution.py:14
  11.5 9.5 %collective-permute-start.1 = (bf16[1,3,64,512]{3,2,1,0:T(8,128)(2,1)}, bf16[1,3,64,512]{3,2,1,0:T(8,128)(2,1)}, u32[]{:S(2)}, u32[]{:S(2)}) collective-permute-start(bf16[1,3,64,512]{3,2,1,0:T(8,128)(2,1)} %bitcast.2), channel_id=1, source_target_pairs={{16,0},{32,16},{48,32},{64,48},{80,64},{96,80},{112,96},{0,112},{1... | collective-permute-start | bytes 589832 | tf_op jit(solution)/shard_map/ppermute | solution.py:16
  17.5 3.0 %copy-start.27 = (f32[256]{0:T(256)}, f32[256]{0:T(256)S(1)}, u32[]{:S(2)}) copy-start(f32[256]{0:T(256)S(1)} %broadcast_multiply_fusion.4) | copy-start | bytes 3076
  22.0 10.9 %collective-permute-start.2 = (bf16[5,1,64,512]{3,2,1,0:T(8,128)(2,1)S(1)}, bf16[5,1,64,512]{3,2,1,0:T(8,128)(2,1)S(1)}, u32[]{:S(2)}, u32[]{:S(2)}) collective-permute-start(bf16[5,1,64,512]{3,2,1,0:T(8,128)(2,1)S(1)} %get-tuple-element.4), channel_id=1, source_target_pairs={{0,1},{1,2},{2,3},{3,4},{4,5},{5,6},{6,7},{7,8},{8,9},{9,10},{10,1... | collective-permute-start | bytes 983048 | tf_op jit(solution)/shard_map/ppermute | solution.py:14
  23.3 9.6 %collective-permute-start.3 = (bf16[5,1,64,512]{3,2,1,0:T(8,128)(2,1)S(1)}, bf16[5,1,64,512]{3,2,1,0:T(8,128)(2,1)S(1)}, u32[]{:S(2)}, u32[]{:S(2)}) collective-permute-start(bf16[5,1,64,512]{3,2,1,0:T(8,128)(2,1)S(1)} %get-tuple-element.5), channel_id=1, source_target_pairs={{1,0},{2,1},{3,2},{4,3},{5,4},{6,5},{7,6},{8,7},{9,8},{10,9},{11,1... | collective-permute-start | bytes 983048 | tf_op jit(solution)/shard_map/ppermute | solution.py:16
  36.3 8.0 %copy-start.8 = (bf16[512,512]{1,0:T(8,128)(2,1)S(1)}, bf16[512,512]{1,0:T(8,128)(2,1)}, u32[]{:S(2)}) copy-start(bf16[512,512]{1,0:T(8,128)(2,1)} %param.55) | copy-start | bytes 1572868
  36.4 8.0 %copy-start.9 = (bf16[512,512]{1,0:T(8,128)(2,1)S(1)}, bf16[512,512]{1,0:T(8,128)(2,1)}, u32[]{:S(2)}) copy-start(bf16[512,512]{1,0:T(8,128)(2,1)} %param.54) | copy-start | bytes 1572868
  36.4 8.0 %copy-start.17 = (f32[64,512]{1,0:T(8,128)S(1)}, f32[64,512]{1,0:T(8,128)}, u32[]{:S(2)}) copy-start(f32[64,512]{1,0:T(8,128)} %fusion.53) | copy-start | bytes 393220
  36.4 8.8 %copy-start.5 = (bf16[64,512]{1,0:T(8,128)(2,1)S(1)}, bf16[64,512]{1,0:T(8,128)(2,1)}, u32[]{:S(2)}) copy-start(bf16[64,512]{1,0:T(8,128)(2,1)} %param.36) | copy-start | bytes 196612
  44.4 1.8 %copy-start.35 = (pred[128]{0:T(512)(128)(4,1)S(1)}, pred[128]{0:T(512)(128)(4,1)}, u32[]{:S(2)}) copy-start(pred[128]{0:T(512)(128)(4,1)} %compare_and_fusion.7) | copy-start | bytes 388
  44.4 6.2 %copy-start.2 = (bf16[512,512]{1,0:T(8,128)(2,1)S(1)}, bf16[512,512]{1,0:T(8,128)(2,1)}, u32[]{:S(2)}) copy-start(bf16[512,512]{1,0:T(8,128)(2,1)} %param.56) | copy-start | bytes 1572868
  44.9 5.9 %copy-start.10 = (bf16[512,512]{1,0:T(8,128)(2,1)S(1)}, bf16[512,512]{1,0:T(8,128)(2,1)}, u32[]{:S(2)}) copy-start(bf16[512,512]{1,0:T(8,128)(2,1)} %param.57) | copy-start | bytes 1572868
  44.9 6.1 %copy-start.31 = (pred[2,2,32]{2,1,0:T(4,128)(4,1)S(1)}, pred[2,2,32]{2,1,0:T(4,128)(4,1)}, u32[]{:S(2)}) copy-start(pred[2,2,32]{2,1,0:T(4,128)(4,1)} %compare_and_fusion.2) | copy-start | bytes 388
  46.4 9.6 %collective-permute-start.4 = (bf16[1,2,32,512]{3,2,1,0:T(8,128)(2,1)S(1)}, bf16[1,2,32,512]{3,2,1,0:T(8,128)(2,1)S(1)}, u32[]{:S(2)}, u32[]{:S(2)}) collective-permute-start(bf16[1,2,32,512]{3,2,1,0:T(8,128)(2,1)S(1)} %bitcast.86), channel_id=1, source_target_pairs={{0,16},{16,32},{32,48},{48,64},{64,80},{80,96},{96,112},{112,0},{1... | collective-permute-start | bytes 196616 | tf_op jit(solution)/shard_map/ppermute | solution.py:14
  50.6 5.4 %collective-permute-start.5 = (bf16[1,2,32,512]{3,2,1,0:T(8,128)(2,1)S(1)}, bf16[1,2,32,512]{3,2,1,0:T(8,128)(2,1)S(1)}, u32[]{:S(2)}, u32[]{:S(2)}) collective-permute-start(bf16[1,2,32,512]{3,2,1,0:T(8,128)(2,1)S(1)} %bitcast.85), channel_id=1, source_target_pairs={{16,0},{32,16},{48,32},{64,48},{80,64},{96,80},{112,96},{0,112},{1... | collective-permute-start | bytes 196616 | tf_op jit(solution)/shard_map/ppermute | solution.py:16
  51.1 10.1 %copy-start.11 = (bf16[512,512]{1,0:T(8,128)(2,1)S(1)}, bf16[512,512]{1,0:T(8,128)(2,1)}, u32[]{:S(2)}) copy-start(bf16[512,512]{1,0:T(8,128)(2,1)} %param.60) | copy-start | bytes 1572868
  56.1 7.3 %collective-permute-start.6 = (bf16[4,1,32,512]{3,2,1,0:T(8,128)(2,1)S(1)}, bf16[4,1,32,512]{3,2,1,0:T(8,128)(2,1)S(1)}, u32[]{:S(2)}, u32[]{:S(2)}) collective-permute-start(bf16[4,1,32,512]{3,2,1,0:T(8,128)(2,1)S(1)} %get-tuple-element.12), channel_id=1, source_target_pairs={{0,1},{1,2},{2,3},{3,4},{4,5},{5,6},{6,7},{7,8},{8,9},{9,10},{10,1... | collective-permute-start | bytes 393224 | tf_op jit(solution)/shard_map/ppermute | solution.py:14
  56.1 7.2 %collective-permute-start.7 = (bf16[4,1,32,512]{3,2,1,0:T(8,128)(2,1)S(1)}, bf16[4,1,32,512]{3,2,1,0:T(8,128)(2,1)S(1)}, u32[]{:S(2)}, u32[]{:S(2)}) collective-permute-start(bf16[4,1,32,512]{3,2,1,0:T(8,128)(2,1)S(1)} %get-tuple-element.13), channel_id=1, source_target_pairs={{1,0},{2,1},{3,2},{4,3},{5,4},{6,5},{7,6},{8,7},{9,8},{10,9},{11,1... | collective-permute-start | bytes 393224 | tf_op jit(solution)/shard_map/ppermute | solution.py:16
  63.9 4.9 %copy-start.33 = (pred[1024]{0:T(1024)(128)(4,1)S(1)}, pred[1024]{0:T(1024)(128)(4,1)}, u32[]{:S(2)}) copy-start(pred[1024]{0:T(1024)(128)(4,1)} %get-tuple-element.38) | copy-start | bytes 3076
  63.9 4.9 %copy-start.34 = (pred[1024]{0:T(1024)(128)(4,1)S(1)}, pred[1024]{0:T(1024)(128)(4,1)}, u32[]{:S(2)}) copy-start(pred[1024]{0:T(1024)(128)(4,1)} %get-tuple-element.39) | copy-start | bytes 3076
  63.9 4.9 %copy-start.38 = (f32[4,1024]{1,0:T(4,128)S(1)}, f32[4,1024]{1,0:T(4,128)}, u32[]{:S(2)}) copy-start(f32[4,1024]{1,0:T(4,128)} %param.43) | copy-start | bytes 49156
  64.0 4.9 %copy-start.39 = (f32[4,512]{1,0:T(4,128)S(1)}, f32[4,512]{1,0:T(4,128)}, u32[]{:S(2)}) copy-start(f32[4,512]{1,0:T(4,128)} %param.58) | copy-start | bytes 24580
  74.7 9.2 %copy-start.12 = (bf16[512,512]{1,0:T(8,128)(2,1)S(1)}, bf16[512,512]{1,0:T(8,128)(2,1)}, u32[]{:S(2)}) copy-start(bf16[512,512]{1,0:T(8,128)(2,1)} %param.62) | copy-start | bytes 1572868
  76.6 9.3 %copy-start.13 = (bf16[512,512]{1,0:T(8,128)(2,1)S(1)}, bf16[512,512]{1,0:T(8,128)(2,1)}, u32[]{:S(2)}) copy-start(bf16[512,512]{1,0:T(8,128)(2,1)} %param.63) | copy-start | bytes 1572868
  85.8 3.0 %copy-start.18 = (bf16[64,512]{1,0:T(8,128)(2,1)}, bf16[64,512]{1,0:T(8,128)(2,1)S(1)}, u32[]{:S(2)}) copy-start(bf16[64,512]{1,0:T(8,128)(2,1)S(1)} %add_convert_fusion.3) | copy-start | bytes 196612
  86.1 2.8 %copy-start.25 = (f32[4,864]{1,0:T(4,128)S(1)}, f32[4,864]{1,0:T(4,128)}, u32[]{:S(2)}) copy-start(f32[4,864]{1,0:T(4,128)} %param.46) | copy-start | bytes 41476
  86.1 2.8 %copy-start.29 = (f32[4,512]{1,0:T(4,128)S(1)}, f32[4,512]{1,0:T(4,128)}, u32[]{:S(2)}) copy-start(f32[4,512]{1,0:T(4,128)} %param.65) | copy-start | bytes 24580
  86.1 2.8 %copy-start.30 = (pred[864]{0:T(1024)(128)(4,1)S(1)}, pred[864]{0:T(1024)(128)(4,1)}, u32[]{:S(2)}) copy-start(pred[864]{0:T(1024)(128)(4,1)} %compare_and_fusion.6) | copy-start | bytes 2596
  88.9 5.2 %copy-start.21 = (s32[864]{0:T(1024)S(1)}, s32[864]{0:T(1024)}, u32[]{:S(2)}) copy-start(s32[864]{0:T(1024)} %param.45) | copy-start | bytes 10372
  88.9 5.2 %copy-start.14 = (bf16[512,512]{1,0:T(8,128)(2,1)S(1)}, bf16[512,512]{1,0:T(8,128)(2,1)}, u32[]{:S(2)}) copy-start(bf16[512,512]{1,0:T(8,128)(2,1)} %param.64) | copy-start | bytes 1572868
  90.7 7.0 %collective-permute-start.8 = (bf16[1,3,96,512]{3,2,1,0:T(8,128)(2,1)S(1)}, bf16[1,3,96,512]{3,2,1,0:T(8,128)(2,1)S(1)}, u32[]{:S(2)}, u32[]{:S(2)}) collective-permute-start(bf16[1,3,96,512]{3,2,1,0:T(8,128)(2,1)S(1)} %bitcast.84), channel_id=1, source_target_pairs={{0,16},{16,32},{32,48},{48,64},{64,80},{80,96},{96,112},{112,0},{1... | collective-permute-start | bytes 884744 | tf_op jit(solution)/shard_map/ppermute | solution.py:14
  94.1 6.3 %collective-permute-start.9 = (bf16[1,3,96,512]{3,2,1,0:T(8,128)(2,1)S(1)}, bf16[1,3,96,512]{3,2,1,0:T(8,128)(2,1)S(1)}, u32[]{:S(2)}, u32[]{:S(2)}) collective-permute-start(bf16[1,3,96,512]{3,2,1,0:T(8,128)(2,1)S(1)} %bitcast.83), channel_id=1, source_target_pairs={{16,0},{32,16},{48,32},{64,48},{80,64},{96,80},{112,96},{0,112},{1... | collective-permute-start | bytes 884744 | tf_op jit(solution)/shard_map/ppermute | solution.py:16
  101.4 16.7 %collective-permute-start.10 = (bf16[5,1,96,512]{3,2,1,0:T(8,128)(2,1)}, bf16[5,1,96,512]{3,2,1,0:T(8,128)(2,1)}, u32[]{:S(2)}, u32[]{:S(2)}) collective-permute-start(bf16[5,1,96,512]{3,2,1,0:T(8,128)(2,1)} %get-tuple-element.2), channel_id=1, source_target_pairs={{0,1},{1,2},{2,3},{3,4},{4,5},{5,6},{6,7},{7,8},{8,9},{9,10},{10,1... | collective-permute-start | bytes 1474568 | tf_op jit(solution)/shard_map/ppermute | solution.py:14
  101.4 16.7 %collective-permute-start.11 = (bf16[5,1,96,512]{3,2,1,0:T(8,128)(2,1)}, bf16[5,1,96,512]{3,2,1,0:T(8,128)(2,1)}, u32[]{:S(2)}, u32[]{:S(2)}) collective-permute-start(bf16[5,1,96,512]{3,2,1,0:T(8,128)(2,1)} %get-tuple-element.3), channel_id=1, source_target_pairs={{1,0},{2,1},{3,2},{4,3},{5,4},{6,5},{7,6},{8,7},{9,8},{10,9},{11,1... | collective-permute-start | bytes 1474568 | tf_op jit(solution)/shard_map/ppermute | solution.py:16
  106.5 3.5 %copy-start.15 = (bf16[512,512]{1,0:T(8,128)(2,1)S(1)}, bf16[512,512]{1,0:T(8,128)(2,1)}, u32[]{:S(2)}) copy-start(bf16[512,512]{1,0:T(8,128)(2,1)} %param.67) | copy-start | bytes 1572868
  (4 other events, 5.3 us)
where the time goes:
time: 136 us; the launch traced here: 135 us
  other arithmetic  40.6 us (30%)
  local copies, waits for them, and re-layouts  27.5 us (20%)
  starting transfers between devices  26 us (19%)
  matrix products  20.8 us (15%)
  waiting for transfers between devices  18.5 us (14%)
  between operations  1.57 us (1%)
    ppermute x6, waiting for transfers between devices, with_halo(): lax.ppermute(tail, axis, [(i, (i + 1) % count) for i in range(count)])  15.9 us
    scatter-add x2, other arithmetic, edge_sum(): jax.ops.segment_sum(message, segment_ids, num_segments=segments + 1)  15.2 us
    ppermute x6, starting transfers between devices, with_halo(): lax.ppermute(head, axis, [((i + 1) % count, i) for i in range(count)])  13.9 us
    dot_general x17, matrix products, project(): return jnp.dot(operand, weights, preferred_element_type=jnp.float32)  13.5 us
    ppermute x6, starting transfers between devices, with_halo(): lax.ppermute(tail, axis, [(i, (i + 1) % count) for i in range(count)])  12.1 us
    scatter-add x1, other arithmetic, process_sum(): return jax.ops.segment_sum(message, targets, num_segments=segments)  7.34 us
    dot_general x3, matrix products, geometry_term(): jnp.einsum('gs,gd->sd', edges, weights, precision=lax.Precision.HIGHEST)  7.29 us
    gather x2, local copies, waits for them, and re-layouts, edge_sum(): jnp.take(target_term, safe_rows, axis=0)  5.71 us
  transfers between devices with their start and end apart: 12, of which 5 were waited for; matrix products, arithmetic and copies ran while one was open for 16% of the time, Pallas kernels for 0%

commit v1 on v0

v1 whole, which is shorter than its diff:
```python
import functools

import jax
import jax.numpy as jnp
from jax import lax
from jax.experimental import pallas as pl
from jax.experimental.pallas import tpu as pltpu
from jax.sharding import PartitionSpec as P

MESH = pl.DeviceIdType.MESH
F32 = jnp.float32
BF16 = jnp.bfloat16
D = 512
GRID = 256
NODES = 64
HALO = 32
ENC = 64
DEC = 96
EDGES = 1024
HALF = EDGES // 2
OFFSETS = [(g // 3 - 1, g % 3 - 1) for g in range(9)]
OTHERS = [g for g in range(9) if g != 4]
CELLS = [
    (-1, -1, 1, 1), (-1, 0, 1, 0), (-1, 0, 1, 1), (-1, 1, 1, 0),
    (0, -1, 0, 1), (0, 1, 0, 0), (0, -1, 1, 1), (0, 1, 1, 0),
    (1, -1, 0, 1), (1, 0, 0, 0), (1, 0, 0, 1), (1, 1, 0, 0),
]

NAMES = [
    "grid_in", "mesh_in", "encode_sources", "encode_targets", "encode_edges", "border_rows",
    "process_sources", "process_targets", "process_edges", "decode_sources", "decode_targets",
    "decode_edges", "refine_hidden", "refine_output", "encode_source", "encode_target",
    "encode_geometry", "encode_output", "mesh_self", "mesh_gather", "mesh_output",
    "process_source", "process_target", "process_geometry", "process_output", "node_self",
    "node_gather", "node_output", "decode_source", "decode_target", "decode_geometry",
    "decode_output", "grid_self", "grid_gather", "grid_output",
]
LOAD_ORDER = [
    "encode_sources", "encode_edges", "encode_geometry", "grid_in", "encode_source",
    "decode_sources", "decode_targets", "decode_edges", "border_rows", "encode_targets",
    "mesh_in", "refine_hidden", "refine_output", "encode_target", "process_sources",
    "process_targets", "process_edges", "process_geometry", "decode_geometry",
    "decode_target", "mesh_self", "grid_self", "encode_output", "mesh_gather", "mesh_output",
    "process_source", "process_target", "process_output", "node_self", "node_gather",
    "node_output", "decode_source", "decode_output", "grid_gather", "grid_output",
]


def dot(left, right):
    return jnp.dot(left, right, preferred_element_type=F32)


def dot_last(left, right):
    return lax.dot_general(left, right, (((1,), (1,)), ((), ())), preferred_element_type=F32)


def silu(values):
    half = 0.5 * values
    return half + half * jnp.tanh(half)


def layer_norm(values):
    average = jnp.mean(values, axis=-1, keepdims=True)
    centred = values - average
    variance = jnp.mean(centred * centred, axis=-1, keepdims=True)
    return centred * lax.rsqrt(variance + 1e-05)


def column_onehot(column, width):
    lanes = lax.broadcasted_iota(jnp.int32, (column.shape[0], width), 1).astype(F32)
    return jnp.where(column == lanes, 1.0, 0.0).astype(BF16)


def row_onehot(row, height):
    rows = lax.broadcasted_iota(jnp.int32, (height, row.shape[1]), 0).astype(F32)
    return jnp.where(row == rows, 1.0, 0.0).astype(BF16)


def split(values):
    high = values.astype(BF16).astype(F32)
    return high, values - high


def geometry_rows(edges):
    high, low = split(edges)
    return jnp.concatenate([high, low, high, jnp.zeros_like(high)], axis=0)


def geometry_weights(weights):
    high, low = split(weights)
    return jnp.concatenate([high, high, low, jnp.zeros_like(high)], axis=0).astype(BF16)


def kernel(n_lat, n_lon, *refs):
    hbm = dict(zip(NAMES, refs[:35]))
    grid_out, mesh_out = refs[35:37]
    vmem = dict(zip(NAMES, refs[37:72]))
    (
        load_sem, out_sem, enc_send_sem, enc_recv_sem, meta_send_sem, meta_recv_sem,
        mesh_send_sem, mesh_recv_sem, back_send_sem, back_recv_sem,
        enc_rows, proc_rows, dec_rows, dec_idx, meta_out, meta_in,
        enc_send, enc_recv, enc_table, enc_tgt_table, enc_tgt_onehot,
        mesh_part, grid_part, refined, dec_table, dec_base, dec_onehot,
        comp, base, near_onehot, proc_tgt_onehot, proc_geo,
        mesh_one, halo_mesh, halo_back, msgs, grid_stage, mesh_stage,
    ) = refs[72:]
    band = lax.axis_index("lat")
    sector = lax.axis_index("lon")

    def peer(g):
        da, db = OFFSETS[g]
        return (lax.rem(band + (da + n_lat), n_lat), lax.rem(sector + (db + n_lon), n_lon))

    loads = {}
    for at, name in enumerate(LOAD_ORDER):
        loads[name] = pltpu.make_async_copy(hbm[name], vmem[name], load_sem.at[at])
        loads[name].start()
    barrier = pltpu.get_barrier_semaphore()
    for g in OTHERS:
        pl.semaphore_signal(barrier, inc=1, device_id=peer(g), device_id_type=MESH)

    def get(name):
        if name in loads:
            loads.pop(name).wait()
        return vmem[name][...]

    def get_row(name):
        return get(name).reshape(1, -1).astype(F32)

    enc_rows[...] = jnp.zeros_like(enc_rows)
    enc_rows[0:1, 0 : 9 * ENC] = get_row("encode_sources")
    enc_rows[8:24, 0 : 9 * ENC] = geometry_rows(get("encode_edges"))
    enc_columns = enc_rows[...].T
    enc_geometry = geometry_weights(get("encode_geometry"))
    enc_table[...] = dot(get("grid_in"), get("encode_source")).astype(BF16)
    pl.semaphore_wait(barrier, 8)
    enc_copies = {}
    for part in (0, 2, 1):
        rows = slice(part * 3 * ENC, (part + 1) * 3 * ENC)
        columns = enc_columns[rows]
        slots = dot(column_onehot(columns[:, 0:1], GRID), enc_table[...]) + dot(
            columns[:, 8:24].astype(BF16), enc_geometry
        )
        enc_send[rows, :] = slots.astype(BF16)
        for g in range(3 * part, 3 * part + 3):
            if g != 4:
                block = pl.ds(g * ENC, ENC)
                enc_copies[g] = pltpu.make_async_remote_copy(
                    src_ref=enc_send.at[block],
                    dst_ref=enc_recv.at[block],
                    send_sem=enc_send_sem.at[g],
                    recv_sem=enc_recv_sem.at[g],
                    device_id=peer(g),
                    device_id_type=MESH,
                )
                enc_copies[g].start()
    enc_recv[4 * ENC : 5 * ENC, :] = enc_send[4 * ENC : 5 * ENC, :]

    dec_idx[...] = jnp.zeros_like(dec_idx)
    dec_idx[0:1, 0 : 9 * DEC] = get_row("decode_sources")
    dec_idx[1:2, 0 : 9 * DEC] = get_row("decode_targets")
    dec_idx[8:24, 0 : 9 * DEC] = geometry_rows(get("decode_edges"))
    cells = get("border_rows").astype(F32)
    border = jnp.concatenate([cells[0, 0:1], cells[0, 1:2], cells[1, 0:1], cells[1, 1:2]], axis=1)
    dec_all = dec_idx[...]
    meta_copies = {}
    for g in range(9):
        packet = dec_all if g == 0 else pltpu.roll(dec_all, dec_all.shape[1] - g * DEC, 1)
        meta_out[g] = packet[:, 0:128]
        meta_out[g, 2:3, :] = border
        if g == 4:
            meta_in[g] = meta_out[g]
            continue
        meta_copies[g] = pltpu.make_async_remote_copy(
            src_ref=meta_out.at[g],
            dst_ref=meta_in.at[g],
            send_sem=meta_send_sem.at[g],
            recv_sem=meta_recv_sem.at[g],
            device_id=peer(g),
            device_id_type=MESH,
        )
        meta_copies[g].start()

    mesh_rows = get("mesh_in")
    enc_target_row = get_row("encode_targets")
    enc_rows[1:2, 0 : 9 * ENC] = enc_target_row
    enc_columns = enc_rows[...].T
    enc_tgt_onehot[...] = column_onehot(enc_columns[0 : 9 * ENC, 1:2], NODES)
    grid_rows = get("grid_in")
    hidden = silu(dot(grid_rows, get("refine_hidden"))).astype(BF16)
    refined[...] = (grid_rows.astype(F32) + layer_norm(dot(hidden, get("refine_output")))).astype(BF16)
    enc_tgt_table[...] = dot(mesh_rows, get("encode_target")).astype(BF16)
    dec_table[...] = dot(refined[...], get("decode_target")).astype(BF16)
    mesh_part[...] = dot(mesh_rows, get("mesh_self"))
    grid_part[...] = dot(refined[...], get("grid_self"))

    proc_rows[...] = jnp.zeros_like(proc_rows)
    proc_rows[0:1, :] = get_row("process_sources")
    proc_target_row = get_row("process_targets")
    proc_rows[1:2, :] = proc_target_row
    proc_rows[8:24, :] = geometry_rows(get("process_edges"))
    proc_columns = proc_rows[...].T
    near_onehot[...] = column_onehot(proc_columns[0:HALF, 0:1], NODES)
    proc_tgt_onehot[...] = column_onehot(proc_columns[:, 1:2], NODES)
    proc_geo[...] = proc_columns[:, 8:24].astype(BF16)
    proc_geometry = geometry_weights(get("process_geometry"))

    for g in OTHERS:
        meta_copies[g].wait_recv()
    dec_columns = dec_idx[...].T
    dec_geometry = geometry_weights(get("decode_geometry"))
    for g in range(9):
        rows = slice(g * DEC, (g + 1) * DEC)
        columns = meta_in[g].T[0:DEC]
        dec_onehot[rows, :] = column_onehot(columns[:, 0:1], NODES)
        dec_base[rows, :] = dot(column_onehot(dec_columns[rows, 1:2], GRID), dec_table[...]) + dot(
            columns[:, 8:24].astype(BF16), dec_geometry
        )
    lane = lax.broadcasted_iota(jnp.int32, (8, 128), 1)
    tiles = []
    for tile in range(3):
        placed = jnp.full((8, 128), -1.0, F32)
        for c in range(4 * tile, 4 * tile + 4):
            da, db, u, v = CELLS[c]
            g = (1 - da) * 3 + (1 - db)
            low = 32 * (c % 4)
            shift = (low - 32 * (2 * u + v)) % 128
            chosen = meta_in[g, 0:8, :]
            if shift:
                chosen = pltpu.roll(chosen, shift, 1)
            chosen = chosen + float(NODES * g)
            if da == -1:
                chosen = jnp.where(band == 0, -1.0, chosen)
            if da == 1:
                chosen = jnp.where(band == n_lat - 1, -1.0, chosen)
            placed = jnp.where((lane >= low) & (lane < low + 32), chosen, placed)
        tiles.append(placed[2:3])
    border_onehot = row_onehot(jnp.concatenate(tiles, axis=1), 9 * NODES)
    for part in range(2):
        rows = slice(part * 256, (part + 1) * 256)
        far = column_onehot(proc_columns[HALF + part * 256 : HALF + (part + 1) * 256, 0:1] - float(NODES), 12 * HALO)
        comp[rows, :] = dot_last(far, border_onehot).astype(BF16)

    for part in (1, 0, 2):
        for g in range(3 * part, 3 * part + 3):
            if g != 4:
                enc_copies[g].wait_recv()
        rows = slice(part * 3 * ENC, (part + 1) * 3 * ENC)
        pre = enc_recv[rows, :].astype(F32) + dot(enc_tgt_onehot[rows, :], enc_tgt_table[...])
        msgs[rows, :] = layer_norm(dot(silu(pre).astype(BF16), get("encode_output"))).astype(BF16)
    total = dot(row_onehot(enc_target_row, NODES), msgs[0 : 9 * ENC, :]).astype(BF16)
    hidden = silu(mesh_part[...] + dot(total, get("mesh_gather"))).astype(BF16)
    mesh_one[...] = (mesh_rows.astype(F32) + layer_norm(dot(hidden, get("mesh_output")))).astype(BF16)

    def spread(halo, send_sem, recv_sem):
        copies = {}
        own = pl.ds(4 * NODES, NODES)
        for g in OTHERS:
            copies[g] = pltpu.make_async_remote_copy(
                src_ref=halo.at[own],
                dst_ref=halo.at[pl.ds(g * NODES, NODES)],
                send_sem=send_sem.at[g],
                recv_sem=recv_sem.at[g],
                device_id=peer(g),
                device_id_type=MESH,
            )
            copies[g].start()
        return copies

    own_rows = slice(4 * NODES, 5 * NODES)
    halo_mesh[own_rows, :] = dot(mesh_one[...], get("process_source")).astype(BF16)
    mesh_copies = spread(halo_mesh, mesh_send_sem, mesh_recv_sem)
    proc_tgt_table = dot(mesh_one[...], get("process_target")).astype(BF16)
    for part in range(4):
        rows = slice(part * 256, (part + 1) * 256)
        base[rows, :] = dot(proc_tgt_onehot[rows, :], proc_tgt_table) + dot(proc_geo[rows, :], proc_geometry)
        if part < 2:
            pre = base[rows, :] + dot(near_onehot[rows, :], halo_mesh[own_rows, :])
            msgs[rows, :] = layer_norm(dot(silu(pre).astype(BF16), get("process_output"))).astype(BF16)
    mesh_part[...] = dot(mesh_one[...], get("node_self"))
    for g in OTHERS:
        mesh_copies[g].wait_recv()
    for part in range(2, 4):
        rows = slice(part * 256, (part + 1) * 256)
        pre = base[rows, :] + dot(comp[(part - 2) * 256 : (part - 1) * 256, :], halo_mesh[...])
        msgs[rows, :] = layer_norm(dot(silu(pre).astype(BF16), get("process_output"))).astype(BF16)
    total = dot(row_onehot(proc_target_row, NODES), msgs[...]).astype(BF16)
    hidden = silu(mesh_part[...] + dot(total, get("node_gather"))).astype(BF16)
    mesh_stage[...] = (mesh_one[...].astype(F32) + layer_norm(dot(hidden, get("node_output")))).astype(BF16)

    halo_back[own_rows, :] = dot(mesh_stage[...], get("decode_source")).astype(BF16)
    back_copies = spread(halo_back, back_send_sem, back_recv_sem)
    mesh_store = pltpu.make_async_copy(mesh_stage, mesh_out, out_sem.at[0])
    mesh_store.start()
    dec_scatter = row_onehot(get_row("decode_targets"), GRID)
    for part in (1, 0, 2):
        for g in range(3 * part, 3 * part + 3):
            if g != 4:
                back_copies[g].wait_recv()
        hidden = []
        for g in range(3 * part, 3 * part + 3):
            rows = slice(g * DEC, (g + 1) * DEC)
            pre = dec_base[rows, :] + dot(dec_onehot[rows, :], halo_back[g * NODES : (g + 1) * NODES, :])
            hidden.append(silu(pre).astype(BF16))
        rows = slice(part * 3 * DEC, (part + 1) * 3 * DEC)
        msgs[rows, :] = layer_norm(dot(jnp.concatenate(hidden, axis=0), get("decode_output"))).astype(BF16)
    total = dot(dec_scatter, msgs[0 : 9 * DEC, :]).astype(BF16)
    hidden = silu(grid_part[...] + dot(total, get("grid_gather"))).astype(BF16)
    grid_stage[...] = (refined[...].astype(F32) + layer_norm(dot(hidden, get("grid_output")))).astype(BF16)
    grid_store = pltpu.make_async_copy(grid_stage, grid_out, out_sem.at[1])
    grid_store.start()
    for copies in (enc_copies, meta_copies, mesh_copies, back_copies):
        for g in OTHERS:
            copies[g].wait_send()
    mesh_store.wait()
    grid_store.wait()


def body(n_lat, n_lon, *arrays):
    dma = pltpu.SemaphoreType.DMA
    vmem = pltpu.VMEM
    scratch = [vmem(x.shape, x.dtype) for x in arrays]
    scratch += [dma((35,)), dma((2,))] + [dma((9,)) for _ in range(8)]
    scratch += [
        vmem((24, 640), F32),
        vmem((24, EDGES), F32),
        vmem((24, 896), F32),
        vmem((24, 896), F32),
        vmem((9, 24, 128), F32),
        vmem((9, 24, 128), F32),
        vmem((9 * ENC, D), BF16),
        vmem((9 * ENC, D), BF16),
        vmem((GRID, D), BF16),
        vmem((NODES, D), BF16),
        vmem((9 * ENC, NODES), BF16),
        vmem((NODES, D), F32),
        vmem((GRID, D), F32),
        vmem((GRID, D), BF16),
        vmem((GRID, D), BF16),
        vmem((9 * DEC, D), F32),
        vmem((9 * DEC, NODES), BF16),
        vmem((HALF, 9 * NODES), BF16),
        vmem((EDGES, D), F32),
        vmem((HALF, NODES), BF16),
        vmem((EDGES, NODES), BF16),
        vmem((EDGES, 16), BF16),
        vmem((NODES, D), BF16),
        vmem((9 * NODES, D), BF16),
        vmem((9 * NODES, D), BF16),
        vmem((EDGES, D), BF16),
        vmem((GRID, D), BF16),
        vmem((NODES, D), BF16),
    ]
    return pl.pallas_call(
        functools.partial(kernel, n_lat, n_lon),
        out_shape=(
            jax.ShapeDtypeStruct((GRID, D), BF16),
            jax.ShapeDtypeStruct((NODES, D), BF16),
        ),
        in_specs=[pl.BlockSpec(memory_space=pl.ANY)] * 35,
        out_specs=[pl.BlockSpec(memory_space=pl.ANY)] * 2,
        scratch_shapes=scratch,
        compiler_params=pltpu.CompilerParams(
            collective_id=0, has_side_effects=True, vmem_limit_bytes=48 * 2**20
        ),
        cost_estimate=pl.CostEstimate(flops=6 * 10**9, bytes_accessed=12 * 10**6, transcendentals=2 * 10**6),
    )(*arrays)


def solution(mesh):
    n_lat, n_lon = mesh.shape["lat"], mesh.shape["lon"]
    rows = P(("lat", "lon"), None)
    line = P(("lat", "lon"))
    edges = P(None, ("lat", "lon"))
    placed = (rows, rows, line, line, edges, P("lat", "lon", None), line, line, edges, line, line, edges)
    placed += (P(),) * 23
    return jax.shard_map(
        functools.partial(body, n_lat, n_lon),
        mesh=mesh,
        in_specs=placed,
        out_specs=(rows, rows),
        check_vma=False,
    )
```

time: 136 us -> 65.8 us (0.48)
  the two profiles are of different devices: /device:TPU:1 before, /device:TPU:0 now
where the time goes in v1:
time: 65.8 us; the launch traced here: 64.7 us
  Pallas kernels  41.5 us (63%)
  local copies, waits for them, and re-layouts  22.5 us (34%)
  between operations  0.68 us (1%)
    pallas_call x1, Pallas kernels, body(): pl.pallas_call(functools.partial(kernel, n_lat, n_lon), out_shape=(jax.Sh...  41.5 us
    unnamed x52, local copies, waits for them, and re-layouts  22.5 us

profile of v1, /device:TPU:0, one launch (start us, length us, event | category | flops | bytes accessed | tf_op | source)
XLA Modules:
  0.0 64.7 jit_solution(8805095427741886151)
XLA Ops:
  0.6 0.0 copy-start
  0.6 1.0 %copy-done = bf16[512,512]{1,0:T(8,128)(2,1)S(1)} copy-done((bf16[512,512]{1,0:T(8,128)(2,1)S(1)}, bf16[512,512]{1,0:T(8,128)(2,1)}, u32[]{:S(2)}) %copy-start) | copy-done | bytes 524312
  1.7 0.0 copy-start.1
  1.7 1.0 %copy-done.1 = bf16[512,512]{1,0:T(8,128)(2,1)S(1)} copy-done((bf16[512,512]{1,0:T(8,128)(2,1)S(1)}, bf16[512,512]{1,0:T(8,128)(2,1)}, u32[]{:S(2)}) %copy-start.1) | copy-done | bytes 524312
  2.7 0.0 copy-start.2
  2.7 1.0 %copy-done.2 = bf16[512,512]{1,0:T(8,128)(2,1)S(1)} copy-done((bf16[512,512]{1,0:T(8,128)(2,1)S(1)}, bf16[512,512]{1,0:T(8,128)(2,1)}, u32[]{:S(2)}) %copy-start.2) | copy-done | bytes 524312
  3.8 0.0 copy-start.3
  3.8 1.0 %copy-done.3 = bf16[512,512]{1,0:T(8,128)(2,1)S(1)} copy-done((bf16[512,512]{1,0:T(8,128)(2,1)S(1)}, bf16[512,512]{1,0:T(8,128)(2,1)}, u32[]{:S(2)}) %copy-start.3) | copy-done | bytes 524312
  4.8 1.0 %copy-done.4 = bf16[512,512]{1,0:T(8,128)(2,1)S(1)} copy-done((bf16[512,512]{1,0:T(8,128)(2,1)S(1)}, bf16[512,512]{1,0:T(8,128)(2,1)}, u32[]{:S(2)}) %copy-start.4) | copy-done | bytes 524312
  5.8 0.0 copy-start.5
  5.9 1.0 %copy-done.5 = bf16[512,512]{1,0:T(8,128)(2,1)S(1)} copy-done((bf16[512,512]{1,0:T(8,128)(2,1)S(1)}, bf16[512,512]{1,0:T(8,128)(2,1)}, u32[]{:S(2)}) %copy-start.5) | copy-done | bytes 524312
  6.9 0.0 copy-start.6
  6.9 1.0 %copy-done.6 = bf16[512,512]{1,0:T(8,128)(2,1)S(1)} copy-done((bf16[512,512]{1,0:T(8,128)(2,1)S(1)}, bf16[512,512]{1,0:T(8,128)(2,1)}, u32[]{:S(2)}) %copy-start.6) | copy-done | bytes 524312
  7.9 0.0 copy-start.7
  7.9 1.0 %copy-done.7 = bf16[512,512]{1,0:T(8,128)(2,1)S(1)} copy-done((bf16[512,512]{1,0:T(8,128)(2,1)S(1)}, bf16[512,512]{1,0:T(8,128)(2,1)}, u32[]{:S(2)}) %copy-start.7) | copy-done | bytes 524312
  9.0 0.0 copy-start.8
  9.0 1.0 %copy-done.8 = bf16[512,512]{1,0:T(8,128)(2,1)S(1)} copy-done((bf16[512,512]{1,0:T(8,128)(2,1)S(1)}, bf16[512,512]{1,0:T(8,128)(2,1)}, u32[]{:S(2)}) %copy-start.8) | copy-done | bytes 524312
  10.0 0.0 copy-start.9
  10.0 1.0 %copy-done.9 = bf16[512,512]{1,0:T(8,128)(2,1)S(1)} copy-done((bf16[512,512]{1,0:T(8,128)(2,1)S(1)}, bf16[512,512]{1,0:T(8,128)(2,1)}, u32[]{:S(2)}) %copy-start.9) | copy-done | bytes 524312
  11.1 0.0 copy-start.10
  11.1 0.9 %copy-done.10 = bf16[256,512]{1,0:T(8,128)(2,1)S(1)} copy-done((bf16[256,512]{1,0:T(8,128)(2,1)S(1)}, bf16[256,512]{1,0:T(8,128)(2,1)}, u32[]{:S(2)}) %copy-start.10) | copy-done | bytes 262168
  12.0 0.0 copy-start.11
  12.0 0.8 %copy-done.11 = bf16[64,512]{1,0:T(8,128)(2,1)S(1)} copy-done((bf16[64,512]{1,0:T(8,128)(2,1)S(1)}, bf16[64,512]{1,0:T(8,128)(2,1)}, u32[]{:S(2)}) %copy-start.11) | copy-done | bytes 65560
  12.9 0.0 copy-start.12
  12.9 0.7 %copy-done.12 = f32[4,1024]{1,0:T(4,128)S(1)} copy-done((f32[4,1024]{1,0:T(4,128)S(1)}, f32[4,1024]{1,0:T(4,128)}, u32[]{:S(2)}) %copy-start.12) | copy-done | bytes 16408
  13.6 0.0 copy-start.13
  13.6 0.7 %copy-done.13 = f32[4,864]{1,0:T(4,128)S(1)} copy-done((f32[4,864]{1,0:T(4,128)S(1)}, f32[4,864]{1,0:T(4,128)}, u32[]{:S(2)}) %copy-start.13) | copy-done | bytes 13848
  14.3 0.0 copy-start.14
  14.3 0.7 %copy-done.14 = f32[4,576]{1,0:T(4,128)S(1)} copy-done((f32[4,576]{1,0:T(4,128)S(1)}, f32[4,576]{1,0:T(4,128)}, u32[]{:S(2)}) %copy-start.14) | copy-done | bytes 9240
  15.0 0.0 copy-start.15
  15.0 0.7 %copy-done.15 = f32[4,512]{1,0:T(4,128)S(1)} copy-done((f32[4,512]{1,0:T(4,128)S(1)}, f32[4,512]{1,0:T(4,128)}, u32[]{:S(2)}) %copy-start.15) | copy-done | bytes 8216
  15.7 0.0 copy-start.16
  15.7 0.7 %copy-done.16 = f32[4,512]{1,0:T(4,128)S(1)} copy-done((f32[4,512]{1,0:T(4,128)S(1)}, f32[4,512]{1,0:T(4,128)}, u32[]{:S(2)}) %copy-start.16) | copy-done | bytes 8216
  16.4 0.0 copy-start.17
  16.4 0.7 %copy-done.17 = f32[4,512]{1,0:T(4,128)S(1)} copy-done((f32[4,512]{1,0:T(4,128)S(1)}, f32[4,512]{1,0:T(4,128)}, u32[]{:S(2)}) %copy-start.17) | copy-done | bytes 8216
  17.1 0.0 copy-start.18
  17.1 0.7 %copy-done.18 = s32[576]{0:T(1024)S(1)} copy-done((s32[576]{0:T(1024)S(1)}, s32[576]{0:T(1024)}, u32[]{:S(2)}) %copy-start.18) | copy-done | bytes 2328
  17.8 0.0 copy-start.19
  17.8 0.7 %copy-done.19 = s32[576]{0:T(1024)S(1)} copy-done((s32[576]{0:T(1024)S(1)}, s32[576]{0:T(1024)}, u32[]{:S(2)}) %copy-start.19) | copy-done | bytes 2328
  18.5 0.0 copy-start.20
  18.5 0.7 %copy-done.20 = s32[1024]{0:T(1024)S(1)} copy-done((s32[1024]{0:T(1024)S(1)}, s32[1024]{0:T(1024)}, u32[]{:S(2)}) %copy-start.20) | copy-done | bytes 4120
  19.1 0.7 %copy-done.21 = s32[1024]{0:T(1024)S(1)} copy-done((s32[1024]{0:T(1024)S(1)}, s32[1024]{0:T(1024)}, u32[]{:S(2)}) %copy-start.21) | copy-done | bytes 4120
  19.8 0.7 %copy-done.22 = s32[864]{0:T(1024)S(1)} copy-done((s32[864]{0:T(1024)S(1)}, s32[864]{0:T(1024)}, u32[]{:S(2)}) %copy-start.22) | copy-done | bytes 3480
  20.5 0.7 %copy-done.23 = s32[864]{0:T(1024)S(1)} copy-done((s32[864]{0:T(1024)S(1)}, s32[864]{0:T(1024)}, u32[]{:S(2)}) %copy-start.23) | copy-done | bytes 3480
  21.2 0.7 %copy-done.24 = s32[2,2,32]{2,1,0:T(2,128)S(1)} copy-done((s32[2,2,32]{2,1,0:T(2,128)S(1)}, s32[2,2,32]{2,1,0:T(2,128)}, u32[]{:S(2)}) %copy-start.24) | copy-done | bytes 536
  21.9 41.5 %shard_map.338 = (bf16[256,512]{1,0:T(8,128)(2,1)S(1)}, bf16[64,512]{1,0:T(8,128)(2,1)S(1)}) custom-call(bf16[256,512]{1,0:T(8,128)(2,1)S(1)} %copy-done.10, bf16[64,512]{1,0:T(8,128)(2,1)S(1)} %copy-done.11, s32[576]{0:T(1024)S(1)} %copy-done.18, s32[576]{0:T(1024)S(1)} %copy-done.19, f32[4,576]{1,0:T(4,128)S(1)} %copy-done.14, s32[2,2,32]{2,1,0:T(2,128)S(1)} %copy-done.24, ...), custom_call_target="tpu_custom_call" | custom-call | flops 6000000000 | bytes 12000000 | tf_op jit(solution)/shard_map/pallas_call | solution.py:354
  63.3 0.7 %copy.39 = bf16[256,512]{1,0:T(8,128)(2,1)} copy(bf16[256,512]{1,0:T(8,128)(2,1)S(1)} %get-tuple-element.4) | data formatting | bytes 524288
  64.1 0.6 copy.40
  (5 shorter events, 0.0 us)
Async XLA Ops:
  0.6 1.0 %copy-start = (bf16[512,512]{1,0:T(8,128)(2,1)S(1)}, bf16[512,512]{1,0:T(8,128)(2,1)}, u32[]{:S(2)}) copy-start(bf16[512,512]{1,0:T(8,128)(2,1)} %refs_12_.1) | copy-start | bytes 1572868
  1.7 1.0 %copy-start.1 = (bf16[512,512]{1,0:T(8,128)(2,1)S(1)}, bf16[512,512]{1,0:T(8,128)(2,1)}, u32[]{:S(2)}) copy-start(bf16[512,512]{1,0:T(8,128)(2,1)} %refs_13_.1) | copy-start | bytes 1572868
  2.7 1.0 %copy-start.2 = (bf16[512,512]{1,0:T(8,128)(2,1)S(1)}, bf16[512,512]{1,0:T(8,128)(2,1)}, u32[]{:S(2)}) copy-start(bf16[512,512]{1,0:T(8,128)(2,1)} %refs_14_.1) | copy-start | bytes 1572868
  3.8 1.0 %copy-start.3 = (bf16[512,512]{1,0:T(8,128)(2,1)S(1)}, bf16[512,512]{1,0:T(8,128)(2,1)}, u32[]{:S(2)}) copy-start(bf16[512,512]{1,0:T(8,128)(2,1)} %refs_15_.1) | copy-start | bytes 1572868
  4.8 1.0 %copy-start.4 = (bf16[512,512]{1,0:T(8,128)(2,1)S(1)}, bf16[512,512]{1,0:T(8,128)(2,1)}, u32[]{:S(2)}) copy-start(bf16[512,512]{1,0:T(8,128)(2,1)} %refs_17_.1) | copy-start | bytes 1572868
  5.8 1.0 %copy-start.5 = (bf16[512,512]{1,0:T(8,128)(2,1)S(1)}, bf16[512,512]{1,0:T(8,128)(2,1)}, u32[]{:S(2)}) copy-start(bf16[512,512]{1,0:T(8,128)(2,1)} %refs_18_.1) | copy-start | bytes 1572868
  6.9 1.0 %copy-start.6 = (bf16[512,512]{1,0:T(8,128)(2,1)S(1)}, bf16[512,512]{1,0:T(8,128)(2,1)}, u32[]{:S(2)}) copy-start(bf16[512,512]{1,0:T(8,128)(2,1)} %refs_19_.1) | copy-start | bytes 1572868
  7.9 1.0 %copy-start.7 = (bf16[512,512]{1,0:T(8,128)(2,1)S(1)}, bf16[512,512]{1,0:T(8,128)(2,1)}, u32[]{:S(2)}) copy-start(bf16[512,512]{1,0:T(8,128)(2,1)} %refs_20_.1) | copy-start | bytes 1572868
  9.0 1.0 %copy-start.8 = (bf16[512,512]{1,0:T(8,128)(2,1)S(1)}, bf16[512,512]{1,0:T(8,128)(2,1)}, u32[]{:S(2)}) copy-start(bf16[512,512]{1,0:T(8,128)(2,1)} %refs_21_.1) | copy-start | bytes 1572868
  10.0 1.0 %copy-start.9 = (bf16[512,512]{1,0:T(8,128)(2,1)S(1)}, bf16[512,512]{1,0:T(8,128)(2,1)}, u32[]{:S(2)}) copy-start(bf16[512,512]{1,0:T(8,128)(2,1)} %refs_22_.1) | copy-start | bytes 1572868
  11.1 0.9 %copy-start.10 = (bf16[256,512]{1,0:T(8,128)(2,1)S(1)}, bf16[256,512]{1,0:T(8,128)(2,1)}, u32[]{:S(2)}) copy-start(bf16[256,512]{1,0:T(8,128)(2,1)} %refs_0_.1) | copy-start | bytes 786436
  12.0 0.8 %copy-start.11 = (bf16[64,512]{1,0:T(8,128)(2,1)S(1)}, bf16[64,512]{1,0:T(8,128)(2,1)}, u32[]{:S(2)}) copy-start(bf16[64,512]{1,0:T(8,128)(2,1)} %refs_1_.1) | copy-start | bytes 196612
  12.9 0.7 %copy-start.12 = (f32[4,1024]{1,0:T(4,128)S(1)}, f32[4,1024]{1,0:T(4,128)}, u32[]{:S(2)}) copy-start(f32[4,1024]{1,0:T(4,128)} %refs_8_.1) | copy-start | bytes 49156
  13.6 0.7 %copy-start.13 = (f32[4,864]{1,0:T(4,128)S(1)}, f32[4,864]{1,0:T(4,128)}, u32[]{:S(2)}) copy-start(f32[4,864]{1,0:T(4,128)} %refs_11_.1) | copy-start | bytes 41476
  14.3 0.7 %copy-start.14 = (f32[4,576]{1,0:T(4,128)S(1)}, f32[4,576]{1,0:T(4,128)}, u32[]{:S(2)}) copy-start(f32[4,576]{1,0:T(4,128)} %refs_4_.1) | copy-start | bytes 27652
  15.0 0.7 %copy-start.15 = (f32[4,512]{1,0:T(4,128)S(1)}, f32[4,512]{1,0:T(4,128)}, u32[]{:S(2)}) copy-start(f32[4,512]{1,0:T(4,128)} %refs_16_.1) | copy-start | bytes 24580
  15.7 0.7 %copy-start.16 = (f32[4,512]{1,0:T(4,128)S(1)}, f32[4,512]{1,0:T(4,128)}, u32[]{:S(2)}) copy-start(f32[4,512]{1,0:T(4,128)} %refs_23_.1) | copy-start | bytes 24580
  16.4 0.7 %copy-start.17 = (f32[4,512]{1,0:T(4,128)S(1)}, f32[4,512]{1,0:T(4,128)}, u32[]{:S(2)}) copy-start(f32[4,512]{1,0:T(4,128)} %refs_30_.1) | copy-start | bytes 24580
  17.1 0.7 %copy-start.18 = (s32[576]{0:T(1024)S(1)}, s32[576]{0:T(1024)}, u32[]{:S(2)}) copy-start(s32[576]{0:T(1024)} %refs_2_.1) | copy-start | bytes 6916
  17.8 0.7 %copy-start.19 = (s32[576]{0:T(1024)S(1)}, s32[576]{0:T(1024)}, u32[]{:S(2)}) copy-start(s32[576]{0:T(1024)} %refs_3_.1) | copy-start | bytes 6916
  18.5 0.7 %copy-start.20 = (s32[1024]{0:T(1024)S(1)}, s32[1024]{0:T(1024)}, u32[]{:S(2)}) copy-start(s32[1024]{0:T(1024)} %refs_6_.1) | copy-start | bytes 12292
  19.1 0.7 %copy-start.21 = (s32[1024]{0:T(1024)S(1)}, s32[1024]{0:T(1024)}, u32[]{:S(2)}) copy-start(s32[1024]{0:T(1024)} %refs_7_.1) | copy-start | bytes 12292
  19.8 0.7 %copy-start.22 = (s32[864]{0:T(1024)S(1)}, s32[864]{0:T(1024)}, u32[]{:S(2)}) copy-start(s32[864]{0:T(1024)} %refs_9_.1) | copy-start | bytes 10372
  20.5 0.7 %copy-start.23 = (s32[864]{0:T(1024)S(1)}, s32[864]{0:T(1024)}, u32[]{:S(2)}) copy-start(s32[864]{0:T(1024)} %refs_10_.1) | copy-start | bytes 10372
  21.2 0.7 %copy-start.24 = (s32[2,2,32]{2,1,0:T(2,128)S(1)}, s32[2,2,32]{2,1,0:T(2,128)}, u32[]{:S(2)}) copy-start(s32[2,2,32]{2,1,0:T(2,128)} %refs_5_.1) | copy-start | bytes 1540

commit v2 on v1

--- a/solution.py
+++ b/solution.py
@@ -1,3 +1,4 @@
+import enum
 import functools
 
 import jax
@@ -26,23 +27,80 @@
     (1, -1, 0, 1), (1, 0, 0, 0), (1, 0, 0, 1), (1, 1, 0, 0),
 ]
 
-NAMES = [
-    "grid_in", "mesh_in", "encode_sources", "encode_targets", "encode_edges", "border_rows",
-    "process_sources", "process_targets", "process_edges", "decode_sources", "decode_targets",
-    "decode_edges", "refine_hidden", "refine_output", "encode_source", "encode_target",
-    "encode_geometry", "encode_output", "mesh_self", "mesh_gather", "mesh_output",
-    "process_source", "process_target", "process_geometry", "process_output", "node_self",
-    "node_gather", "node_output", "decode_source", "decode_target", "decode_geometry",
-    "decode_output", "grid_self", "grid_gather", "grid_output",
-]
+class Arg(enum.IntEnum):
+    grid_in = 0
+    mesh_in = 1
+    encode_sources = 2
+    encode_targets = 3
+    encode_edges = 4
+    border_rows = 5
+    process_sources = 6
+    process_targets = 7
+    process_edges = 8
+    decode_sources = 9
+    decode_targets = 10
+    decode_edges = 11
+    refine_hidden = 12
+    refine_output = 13
+    encode_source = 14
+    encode_target = 15
+    encode_geometry = 16
+    encode_output = 17
+    mesh_self = 18
+    mesh_gather = 19
+    mesh_output = 20
+    process_source = 21
+    process_target = 22
+    process_geometry = 23
+    process_output = 24
+    node_self = 25
+    node_gather = 26
+    node_output = 27
+    decode_source = 28
+    decode_target = 29
+    decode_geometry = 30
+    decode_output = 31
+    grid_self = 32
+    grid_gather = 33
+    grid_output = 34
+
+
 LOAD_ORDER = [
-    "encode_sources", "encode_edges", "encode_geometry", "grid_in", "encode_source",
-    "decode_sources", "decode_targets", "decode_edges", "border_rows", "encode_targets",
-    "mesh_in", "refine_hidden", "refine_output", "encode_target", "process_sources",
-    "process_targets", "process_edges", "process_geometry", "decode_geometry",
-    "decode_target", "mesh_self", "grid_self", "encode_output", "mesh_gather", "mesh_output",
-    "process_source", "process_target", "process_output", "node_self", "node_gather",
-    "node_output", "decode_source", "decode_output", "grid_gather", "grid_output",
+    Arg.encode_sources,
+    Arg.encode_edges,
+    Arg.encode_geometry,
+    Arg.grid_in,
+    Arg.encode_source,
+    Arg.decode_sources,
+    Arg.decode_targets,
+    Arg.decode_edges,
+    Arg.border_rows,
+    Arg.encode_targets,
+    Arg.mesh_in,
+    Arg.refine_hidden,
+    Arg.refine_output,
+    Arg.encode_target,
+    Arg.process_sources,
+    Arg.process_targets,
+    Arg.process_edges,
+    Arg.process_geometry,
+    Arg.decode_geometry,
+    Arg.decode_target,
+    Arg.mesh_self,
+    Arg.grid_self,
+    Arg.encode_output,
+    Arg.mesh_gather,
+    Arg.mesh_output,
+    Arg.process_source,
+    Arg.process_target,
+    Arg.process_output,
+    Arg.node_self,
+    Arg.node_gather,
+    Arg.node_output,
+    Arg.decode_source,
+    Arg.decode_output,
+    Arg.grid_gather,
+    Arg.grid_output,
 ]
 
 
@@ -92,9 +150,9 @@
 
 
 def kernel(n_lat, n_lon, *refs):
-    hbm = dict(zip(NAMES, refs[:35]))
+    hbm = dict(zip(Arg, refs[:35]))
     grid_out, mesh_out = refs[35:37]
-    vmem = dict(zip(NAMES, refs[37:72]))
+    vmem = dict(zip(Arg, refs[37:72]))
     (
         load_sem, out_sem, enc_send_sem, enc_recv_sem, meta_send_sem, meta_recv_sem,
         mesh_send_sem, mesh_recv_sem, back_send_sem, back_recv_sem,
@@ -128,11 +186,11 @@
         return get(name).reshape(1, -1).astype(F32)
 
     enc_rows[...] = jnp.zeros_like(enc_rows)
-    enc_rows[0:1, 0 : 9 * ENC] = get_row("encode_sources")
-    enc_rows[8:24, 0 : 9 * ENC] = geometry_rows(get("encode_edges"))
+    enc_rows[0:1, 0 : 9 * ENC] = get_row(Arg.encode_sources)
+    enc_rows[8:24, 0 : 9 * ENC] = geometry_rows(get(Arg.encode_edges))
     enc_columns = enc_rows[...].T
-    enc_geometry = geometry_weights(get("encode_geometry"))
-    enc_table[...] = dot(get("grid_in"), get("encode_source")).astype(BF16)
+    enc_geometry = geometry_weights(get(Arg.encode_geometry))
+    enc_table[...] = dot(get(Arg.grid_in), get(Arg.encode_source)).astype(BF16)
     pl.semaphore_wait(barrier, 8)
     enc_copies = {}
     for part in (0, 2, 1):
@@ -157,10 +215,10 @@
     enc_recv[4 * ENC : 5 * ENC, :] = enc_send[4 * ENC : 5 * ENC, :]
 
     dec_idx[...] = jnp.zeros_like(dec_idx)
-    dec_idx[0:1, 0 : 9 * DEC] = get_row("decode_sources")
-    dec_idx[1:2, 0 : 9 * DEC] = get_row("decode_targets")
-    dec_idx[8:24, 0 : 9 * DEC] = geometry_rows(get("decode_edges"))
-    cells = get("border_rows").astype(F32)
+    dec_idx[0:1, 0 : 9 * DEC] = get_row(Arg.decode_sources)
+    dec_idx[1:2, 0 : 9 * DEC] = get_row(Arg.decode_targets)
+    dec_idx[8:24, 0 : 9 * DEC] = geometry_rows(get(Arg.decode_edges))
+    cells = get(Arg.border_rows).astype(F32)
     border = jnp.concatenate([cells[0, 0:1], cells[0, 1:2], cells[1, 0:1], cells[1, 1:2]], axis=1)
     dec_all = dec_idx[...]
     meta_copies = {}
@@ -181,34 +239,34 @@
         )
         meta_copies[g].start()
 
-    mesh_rows = get("mesh_in")
-    enc_target_row = get_row("encode_targets")
+    mesh_rows = get(Arg.mesh_in)
+    enc_target_row = get_row(Arg.encode_targets)
     enc_rows[1:2, 0 : 9 * ENC] = enc_target_row
     enc_columns = enc_rows[...].T
     enc_tgt_onehot[...] = column_onehot(enc_columns[0 : 9 * ENC, 1:2], NODES)
-    grid_rows = get("grid_in")
-    hidden = silu(dot(grid_rows, get("refine_hidden"))).astype(BF16)
-    refined[...] = (grid_rows.astype(F32) + layer_norm(dot(hidden, get("refine_output")))).astype(BF16)
-    enc_tgt_table[...] = dot(mesh_rows, get("encode_target")).astype(BF16)
-    dec_table[...] = dot(refined[...], get("decode_target")).astype(BF16)
-    mesh_part[...] = dot(mesh_rows, get("mesh_self"))
-    grid_part[...] = dot(refined[...], get("grid_self"))
+    grid_rows = get(Arg.grid_in)
+    hidden = silu(dot(grid_rows, get(Arg.refine_hidden))).astype(BF16)
+    refined[...] = (grid_rows.astype(F32) + layer_norm(dot(hidden, get(Arg.refine_output)))).astype(BF16)
+    enc_tgt_table[...] = dot(mesh_rows, get(Arg.encode_target)).astype(BF16)
+    dec_table[...] = dot(refined[...], get(Arg.decode_target)).astype(BF16)
+    mesh_part[...] = dot(mesh_rows, get(Arg.mesh_self))
+    grid_part[...] = dot(refined[...], get(Arg.grid_self))
 
     proc_rows[...] = jnp.zeros_like(proc_rows)
-    proc_rows[0:1, :] = get_row("process_sources")
-    proc_target_row = get_row("process_targets")
+    proc_rows[0:1, :] = get_row(Arg.process_sources)
+    proc_target_row = get_row(Arg.process_targets)
     proc_rows[1:2, :] = proc_target_row
-    proc_rows[8:24, :] = geometry_rows(get("process_edges"))
+    proc_rows[8:24, :] = geometry_rows(get(Arg.process_edges))
     proc_columns = proc_rows[...].T
     near_onehot[...] = column_onehot(proc_columns[0:HALF, 0:1], NODES)
     proc_tgt_onehot[...] = column_onehot(proc_columns[:, 1:2], NODES)
     proc_geo[...] = proc_columns[:, 8:24].astype(BF16)
-    proc_geometry = geometry_weights(get("process_geometry"))
+    proc_geometry = geometry_weights(get(Arg.process_geometry))
 
     for g in OTHERS:
         meta_copies[g].wait_recv()
     dec_columns = dec_idx[...].T
-    dec_geometry = geometry_weights(get("decode_geometry"))
+    dec_geometry = geometry_weights(get(Arg.decode_geometry))
     for g in range(9):
         rows = slice(g * DEC, (g + 1) * DEC)
         columns = meta_in[g].T[0:DEC]
@@ -247,10 +305,10 @@
                 enc_copies[g].wait_recv()
         rows = slice(part * 3 * ENC, (part + 1) * 3 * ENC)
         pre = enc_recv[rows, :].astype(F32) + dot(enc_tgt_onehot[rows, :], enc_tgt_table[...])
-        msgs[rows, :] = layer_norm(dot(silu(pre).astype(BF16), get("encode_output"))).astype(BF16)
+        msgs[rows, :] = layer_norm(dot(silu(pre).astype(BF16), get(Arg.encode_output))).astype(BF16)
     total = dot(row_onehot(enc_target_row, NODES), msgs[0 : 9 * ENC, :]).astype(BF16)
-    hidden = silu(mesh_part[...] + dot(total, get("mesh_gather"))).astype(BF16)
-    mesh_one[...] = (mesh_rows.astype(F32) + layer_norm(dot(hidden, get("mesh_output")))).astype(BF16)
+    hidden = silu(mesh_part[...] + dot(total, get(Arg.mesh_gather))).astype(BF16)
+    mesh_one[...] = (mesh_rows.astype(F32) + layer_norm(dot(hidden, get(Arg.mesh_output)))).astype(BF16)
 
     def spread(halo, send_sem, recv_sem):
         copies = {}
@@ -268,31 +326,31 @@
         return copies
 
     own_rows = slice(4 * NODES, 5 * NODES)
-    halo_mesh[own_rows, :] = dot(mesh_one[...], get("process_source")).astype(BF16)
+    halo_mesh[own_rows, :] = dot(mesh_one[...], get(Arg.process_source)).astype(BF16)
     mesh_copies = spread(halo_mesh, mesh_send_sem, mesh_recv_sem)
-    proc_tgt_table = dot(mesh_one[...], get("process_target")).astype(BF16)
+    proc_tgt_table = dot(mesh_one[...], get(Arg.process_target)).astype(BF16)
     for part in range(4):
         rows = slice(part * 256, (part + 1) * 256)
         base[rows, :] = dot(proc_tgt_onehot[rows, :], proc_tgt_table) + dot(proc_geo[rows, :], proc_geometry)
         if part < 2:
             pre = base[rows, :] + dot(near_onehot[rows, :], halo_mesh[own_rows, :])
-            msgs[rows, :] = layer_norm(dot(silu(pre).astype(BF16), get("process_output"))).astype(BF16)
-    mesh_part[...] = dot(mesh_one[...], get("node_self"))
+            msgs[rows, :] = layer_norm(dot(silu(pre).astype(BF16), get(Arg.process_output))).astype(BF16)
+    mesh_part[...] = dot(mesh_one[...], get(Arg.node_self))
     for g in OTHERS:
         mesh_copies[g].wait_recv()
     for part in range(2, 4):
         rows = slice(part * 256, (part + 1) * 256)
         pre = base[rows, :] + dot(comp[(part - 2) * 256 : (part - 1) * 256, :], halo_mesh[...])
-        msgs[rows, :] = layer_norm(dot(silu(pre).astype(BF16), get("process_output"))).astype(BF16)
+        msgs[rows, :] = layer_norm(dot(silu(pre).astype(BF16), get(Arg.process_output))).astype(BF16)
     total = dot(row_onehot(proc_target_row, NODES), msgs[...]).astype(BF16)
-    hidden = silu(mesh_part[...] + dot(total, get("node_gather"))).astype(BF16)
-    mesh_stage[...] = (mesh_one[...].astype(F32) + layer_norm(dot(hidden, get("node_output")))).astype(BF16)
-
-    halo_back[own_rows, :] = dot(mesh_stage[...], get("decode_source")).astype(BF16)
+    hidden = silu(mesh_part[...] + dot(total, get(Arg.node_gather))).astype(BF16)
+    mesh_stage[...] = (mesh_one[...].astype(F32) + layer_norm(dot(hidden, get(Arg.node_output)))).astype(BF16)
+
+    halo_back[own_rows, :] = dot(mesh_stage[...], get(Arg.decode_source)).astype(BF16)
     back_copies = spread(halo_back, back_send_sem, back_recv_sem)
     mesh_store = pltpu.make_async_copy(mesh_stage, mesh_out, out_sem.at[0])
     mesh_store.start()
-    dec_scatter = row_onehot(get_row("decode_targets"), GRID)
+    dec_scatter = row_onehot(get_row(Arg.decode_targets), GRID)
     for part in (1, 0, 2):
         for g in range(3 * part, 3 * part + 3):
             if g != 4:
@@ -303,10 +361,10 @@
             pre = dec_base[rows, :] + dot(dec_onehot[rows, :], halo_back[g * NODES : (g + 1) * NODES, :])
             hidden.append(silu(pre).astype(BF16))
         rows = slice(part * 3 * DEC, (part + 1) * 3 * DEC)
-        msgs[rows, :] = layer_norm(dot(jnp.concatenate(hidden, axis=0), get("decode_output"))).astype(BF16)
+        msgs[rows, :] = layer_norm(dot(jnp.concatenate(hidden, axis=0), get(Arg.decode_output))).astype(BF16)
     total = dot(dec_scatter, msgs[0 : 9 * DEC, :]).astype(BF16)
-    hidden = silu(grid_part[...] + dot(total, get("grid_gather"))).astype(BF16)
-    grid_stage[...] = (refined[...].astype(F32) + layer_norm(dot(hidden, get("grid_output")))).astype(BF16)
+    hidden = silu(grid_part[...] + dot(total, get(Arg.grid_gather))).astype(BF16)
+    grid_stage[...] = (refined[...].astype(F32) + layer_norm(dot(hidden, get(Arg.grid_output)))).astype(BF16)
     grid_store = pltpu.make_async_copy(grid_stage, grid_out, out_sem.at[1])
     grid_store.start()
     for copies in (enc_copies, meta_copies, mesh_copies, back_copies):
@@ -361,7 +419,7 @@
         out_specs=[pl.BlockSpec(memory_space=pl.ANY)] * 2,
         scratch_shapes=scratch,
         compiler_params=pltpu.CompilerParams(
-            collective_id=0, has_side_effects=True, vmem_limit_bytes=48 * 2**20
+            collective_id=0, has_side_effects=True, vmem_limit_bytes=60 * 2**20
         ),
         cost_estimate=pl.CostEstimate(flops=6 * 10**9, bytes_accessed=12 * 10**6, transcendentals=2 * 10**6),
     )(*arrays)

time: 65.8 us -> 45 us (0.68); the launches traced: 64.7 us -> 44.9 us
  local copies, waits for them, and re-layouts: 22.5 us -> 2.33 us
    unnamed x52 -> x4, local copies, waits for them, and re-layouts: 22.5 us -> 2.33 us
where the time goes in v2:
time: 45 us; the launch traced here: 44.9 us
  Pallas kernels  41.9 us (93%)
  local copies, waits for them, and re-layouts  2.33 us (5%)
  between operations  0.66 us (1%)
    pallas_call x1, Pallas kernels, body(): pl.pallas_call(functools.partial(kernel, n_lat, n_lon), out_shape=(jax.Sh...  41.9 us
    unnamed x4, local copies, waits for them, and re-layouts  2.33 us

profile of v2, /device:TPU:0, one launch (start us, length us, event | category | flops | bytes accessed | tf_op | source)
XLA Modules:
  0.0 44.9 jit_solution(12599637288219875615)
XLA Ops:
  0.6 41.9 %shard_map.338 = (bf16[256,512]{1,0:T(8,128)(2,1)}, bf16[64,512]{1,0:T(8,128)(2,1)}) custom-call(bf16[256,512]{1,0:T(8,128)(2,1)} %refs_0_.1, bf16[64,512]{1,0:T(8,128)(2,1)} %refs_1_.1, s32[576]{0:T(1024)} %refs_2_.1, s32[576]{0:T(1024)} %refs_3_.1, f32[4,576]{1,0:T(4,128)} %refs_4_.1, s32[2,2,32]{2,1,0:T(2,128)} %refs_5_.1, s32[1024]{0:T(1024)} %refs_6_.1, ...), custom_call_target="tpu_custom_call" | custom-call | flops 6000000000 | bytes 12000000 | tf_op jit(solution)/shard_map/pallas_call | solution.py:412
  42.6 0.0 copy-start
  42.6 1.7 %copy.39 = bf16[256,512]{1,0:T(8,128)(2,1)} copy(bf16[256,512]{1,0:T(8,128)(2,1)} %get-tuple-element.4) | data formatting | bytes 524288
  44.3 0.0 copy-done
  44.3 0.6 %copy.40 = bf16[64,512]{1,0:T(8,128)(2,1)} copy(bf16[64,512]{1,0:T(8,128)(2,1)S(1)} %copy-done) | data formatting | bytes 131072
Async XLA Ops:
  42.6 1.7 %copy-start = (bf16[64,512]{1,0:T(8,128)(2,1)S(1)}, bf16[64,512]{1,0:T(8,128)(2,1)}, u32[]{:S(2)}) copy-start(bf16[64,512]{1,0:T(8,128)(2,1)} %get-tuple-element.5) | copy-start | bytes 196612

commit v3 on v2

v3 whole, which is shorter than its diff:
```python
import enum
import functools

import jax
import jax.numpy as jnp
from jax import lax
from jax.experimental import pallas as pl
from jax.experimental.pallas import tpu as pltpu
from jax.sharding import PartitionSpec as P

MESH = pl.DeviceIdType.MESH
F32 = jnp.float32
BF16 = jnp.bfloat16
D = 512
GRID = 256
NODES = 64
HALO = 32
ENC = 64
DEC = 96
EDGES = 1024
HALF = EDGES // 2
OFFSETS = [(g // 3 - 1, g % 3 - 1) for g in range(9)]
OTHERS = [g for g in range(9) if g != 4]
CELLS = [
    (-1, -1, 1, 1), (-1, 0, 1, 0), (-1, 0, 1, 1), (-1, 1, 1, 0),
    (0, -1, 0, 1), (0, 1, 0, 0), (0, -1, 1, 1), (0, 1, 1, 0),
    (1, -1, 0, 1), (1, 0, 0, 0), (1, 0, 0, 1), (1, 1, 0, 0),
]

class Arg(enum.IntEnum):
    grid_in = 0
    mesh_in = 1
    encode_sources = 2
    encode_targets = 3
    encode_edges = 4
    border_rows = 5
    process_sources = 6
    process_targets = 7
    process_edges = 8
    decode_sources = 9
    decode_targets = 10
    decode_edges = 11
    refine_hidden = 12
    refine_output = 13
    encode_source = 14
    encode_target = 15
    encode_geometry = 16
    encode_output = 17
    mesh_self = 18
    mesh_gather = 19
    mesh_output = 20
    process_source = 21
    process_target = 22
    process_geometry = 23
    process_output = 24
    node_self = 25
    node_gather = 26
    node_output = 27
    decode_source = 28
    decode_target = 29
    decode_geometry = 30
    decode_output = 31
    grid_self = 32
    grid_gather = 33
    grid_output = 34


KINDS = [(0, 0), (1, 0), (2, 0), (0, 1), (0, -1), (1, 1), (1, -1), (2, 1), (2, -1)]
MIRROR = [0, 1, 2, 4, 3, 6, 5, 8, 7]
FIRST = [
    Arg.encode_sources,
    Arg.encode_targets,
    Arg.encode_edges,
    Arg.encode_geometry,
    Arg.grid_in,
    Arg.encode_source,
]
SECOND = [
    Arg.decode_sources,
    Arg.decode_targets,
    Arg.decode_edges,
    Arg.border_rows,
    Arg.process_sources,
    Arg.process_targets,
    Arg.process_edges,
    Arg.process_geometry,
    Arg.decode_geometry,
]
THIRD = [
    Arg.refine_hidden,
    Arg.refine_output,
    Arg.mesh_in,
    Arg.decode_target,
    Arg.grid_self,
    Arg.encode_target,
    Arg.mesh_self,
    Arg.encode_output,
    Arg.mesh_gather,
    Arg.mesh_output,
    Arg.process_source,
    Arg.process_target,
    Arg.process_output,
    Arg.node_self,
    Arg.node_gather,
    Arg.node_output,
    Arg.decode_source,
    Arg.decode_output,
    Arg.grid_gather,
    Arg.grid_output,
]


def dot(left, right):
    return jnp.dot(left, right, preferred_element_type=F32)


def dot_last(left, right):
    return lax.dot_general(left, right, (((1,), (1,)), ((), ())), preferred_element_type=F32)


def silu(values):
    half = 0.5 * values
    return half + half * jnp.tanh(half)


def layer_norm(values):
    average = jnp.mean(values, axis=-1, keepdims=True)
    centred = values - average
    variance = jnp.mean(centred * centred, axis=-1, keepdims=True)
    return centred * lax.rsqrt(variance + 1e-05)


def column_onehot(column, width):
    lanes = lax.broadcasted_iota(jnp.int32, (column.shape[0], width), 1).astype(F32)
    return jnp.where(column == lanes, 1.0, 0.0).astype(BF16)


def row_onehot(row, height):
    rows = lax.broadcasted_iota(jnp.int32, (height, row.shape[1]), 0).astype(F32)
    return jnp.where(row == rows, 1.0, 0.0).astype(BF16)


def split(values):
    high = values.astype(BF16).astype(F32)
    return high, values - high


def geometry_rows(edges):
    high, low = split(edges)
    return jnp.concatenate([high, low, high, jnp.zeros_like(high)], axis=0)


def geometry_weights(weights):
    high, low = split(weights)
    return jnp.concatenate([high, high, low, jnp.zeros_like(high)], axis=0).astype(BF16)


def kernel(n_lat, n_lon, *refs):
    hbm = dict(zip(Arg, refs[:35]))
    grid_out, mesh_out = refs[35:37]
    vmem = dict(zip(Arg, refs[37:72]))
    (
        load_sem, enc_send_sem, enc_recv_sem, meta_send_sem, meta_recv_sem,
        mesh_send_sem, mesh_recv_sem, back_send_sem, back_recv_sem,
        enc_rows, enc_cols, proc_rows, dec_rows, dec_cols, meta_out, meta_in,
        enc_send, enc_recv, enc_table, enc_tgt_table, enc_tgt_onehot,
        mesh_part, grid_part, refined, dec_table, dec_base, dec_onehot,
        comp, base, near_onehot, proc_tgt_onehot, proc_geo,
        mesh_one, halo_mesh, halo_back, msgs,
    ) = refs[72:]
    band = lax.axis_index("lat")
    sector = lax.axis_index("lon")
    even = lax.rem(band, 2) == 0
    inner = (band > 0) & (band < n_lat - 1)
    steps = (0, jnp.where(even, 1, -1), jnp.where(even, -1, 1))

    def device(da, db):
        return (lax.rem(band + (da + n_lat), n_lat), lax.rem(sector + (db + n_lon), n_lon))

    def place(kind):
        vertical, db = KINDS[kind]
        return steps[vertical], db

    def arrival_group(kind):
        da, db = place(kind)
        return (1 - da) * 3 + (1 - db)

    def slot_of(da, db):
        if da == 0:
            return KINDS.index((0, db))
        return jnp.where(steps[1] == da, KINDS.index((1, db)), KINDS.index((2, db)))

    def reaches(da):
        return None if da == 0 else (band > 0 if da < 0 else band < n_lat - 1)

    def when(condition, action):
        if condition is None:
            action()
        else:
            pl.when(condition)(action)

    loads = {}

    def load(names):
        for name in names:
            loads[name] = pltpu.make_async_copy(hbm[name], vmem[name], load_sem.at[int(name)])
            loads[name].start()

    def get(name):
        if name in loads:
            loads.pop(name).wait()
        return vmem[name][...]

    def get_row(name):
        return get(name).reshape(1, -1).astype(F32)

    load(FIRST)
    barrier = pltpu.get_barrier_semaphore()
    for g in OTHERS:
        da, db = OFFSETS[g]

        def greet(da=da, db=db):
            pl.semaphore_signal(barrier, inc=1, device_id=device(da, db), device_id_type=MESH)

        when(reaches(da), greet)
    load(SECOND)

    @pl.when(jnp.logical_not(inner))
    def _():
        for kind in range(9):
            if KINDS[kind][0] == 2:
                enc_recv[kind * ENC : (kind + 1) * ENC, :] = jnp.zeros((ENC, D), BF16)
                halo_mesh[kind * NODES : (kind + 1) * NODES, :] = jnp.zeros((NODES, D), BF16)
                halo_back[kind * NODES : (kind + 1) * NODES, :] = jnp.zeros((NODES, D), BF16)
                meta_in[kind] = jnp.zeros((24, 128), F32)

    enc_rows[...] = jnp.zeros_like(enc_rows)
    enc_rows[0:1, 0 : 9 * ENC] = get_row(Arg.encode_sources)
    enc_rows[1:2, 0 : 9 * ENC] = get_row(Arg.encode_targets)
    enc_rows[8:24, 0 : 9 * ENC] = geometry_rows(get(Arg.encode_edges))
    enc_columns = enc_rows[...].T
    enc_cols[...] = enc_columns
    enc_geometry = geometry_weights(get(Arg.encode_geometry))
    enc_table[...] = dot(get(Arg.grid_in), get(Arg.encode_source)).astype(BF16)
    load(THIRD)
    slots = []
    for part in range(3):
        rows = slice(part * 3 * ENC, (part + 1) * 3 * ENC)
        columns = enc_columns[rows]
        enc_send[rows, :] = (
            dot(column_onehot(columns[:, 0:1], GRID), enc_table[...])
            + dot(columns[:, 8:24].astype(BF16), enc_geometry)
        ).astype(BF16)
        if part == 0:
            pl.semaphore_wait(barrier, jnp.where(inner, 8, 5))
        for g in range(3 * part, 3 * part + 3):
            if g == 4:
                enc_recv[0:ENC, :] = enc_send[g * ENC : (g + 1) * ENC, :]
                continue
            da, db = OFFSETS[g]

            def send(da=da, db=db, g=g):
                enc_copy(da, db, g).start()

            def enc_copy(da, db, g):
                slot = slot_of(-da, -db) if da == 0 else jnp.where(
                    steps[1] == da, KINDS.index((1, -db)), KINDS.index((2, -db))
                )
                return pltpu.make_async_remote_copy(
                    src_ref=enc_send.at[pl.ds(g * ENC, ENC)],
                    dst_ref=enc_recv.at[pl.ds(pl.multiple_of(slot * ENC, ENC), ENC)],
                    send_sem=enc_send_sem.at[g],
                    recv_sem=enc_recv_sem.at[slot],
                    device_id=device(da, db),
                    device_id_type=MESH,
                )

            when(reaches(da), send)

    dec_rows[...] = jnp.zeros_like(dec_rows)
    dec_rows[0:1, 0 : 9 * DEC] = get_row(Arg.decode_sources)
    dec_rows[1:2, 0 : 9 * DEC] = get_row(Arg.decode_targets)
    dec_rows[8:24, 0 : 9 * DEC] = geometry_rows(get(Arg.decode_edges))
    cells = get(Arg.border_rows).astype(F32)
    border = jnp.concatenate([cells[0, 0:1], cells[0, 1:2], cells[1, 0:1], cells[1, 1:2]], axis=1)
    dec_all = dec_rows[...]
    for g in range(9):
        packet = dec_all if g == 0 else pltpu.roll(dec_all, dec_all.shape[1] - g * DEC, 1)
        meta_out[g] = packet[:, 0:128]
        meta_out[g, 2:3, :] = border
        if g == 4:
            meta_in[0] = meta_out[g]
            continue
        da, db = OFFSETS[g]

        def meta_copy(da, db, g):
            slot = slot_of(-da, -db) if da == 0 else jnp.where(
                steps[1] == da, KINDS.index((1, -db)), KINDS.index((2, -db))
            )
            return pltpu.make_async_remote_copy(
                src_ref=meta_out.at[g],
                dst_ref=meta_in.at[slot],
                send_sem=meta_send_sem.at[g],
                recv_sem=meta_recv_sem.at[slot],
                device_id=device(da, db),
                device_id_type=MESH,
            )

        def send_meta(da=da, db=db, g=g):
            meta_copy(da, db, g).start()

        when(reaches(da), send_meta)
    dec_cols[...] = dec_all.T

    grid_rows = get(Arg.grid_in)
    hidden = silu(dot(grid_rows, get(Arg.refine_hidden))).astype(BF16)
    refined[...] = (grid_rows.astype(F32) + layer_norm(dot(hidden, get(Arg.refine_output)))).astype(BF16)
    dec_table[...] = dot(refined[...], get(Arg.decode_target)).astype(BF16)
    grid_part[...] = dot(refined[...], get(Arg.grid_self))
    mesh_rows = get(Arg.mesh_in)
    enc_tgt_table[...] = dot(mesh_rows, get(Arg.encode_target)).astype(BF16)
    mesh_part[...] = dot(mesh_rows, get(Arg.mesh_self))
    for kind in range(9):
        group = pl.multiple_of(arrival_group(kind) * ENC, ENC)
        enc_tgt_onehot[kind * ENC : (kind + 1) * ENC, :] = column_onehot(
            enc_cols[pl.ds(group, ENC), 1:2], NODES
        )

    proc_rows[...] = jnp.zeros_like(proc_rows)
    proc_rows[0:1, :] = get_row(Arg.process_sources)
    proc_target_row = get_row(Arg.process_targets)
    proc_rows[1:2, :] = proc_target_row
    proc_rows[8:24, :] = geometry_rows(get(Arg.process_edges))
    proc_columns = proc_rows[...].T
    near_onehot[...] = column_onehot(proc_columns[0:HALF, 0:1], NODES)
    proc_tgt_onehot[...] = column_onehot(proc_columns[:, 1:2], NODES)
    proc_geo[...] = proc_columns[:, 8:24].astype(BF16)
    proc_geometry = geometry_weights(get(Arg.process_geometry))

    def arrived(ref, size, sem, kind):
        block = ref.at[kind] if size is None else ref.at[pl.ds(kind * size, size)]
        pltpu.make_async_remote_copy(
            src_ref=block,
            dst_ref=block,
            send_sem=enc_send_sem.at[kind],
            recv_sem=sem.at[kind],
            device_id=device(*place(1)),
            device_id_type=MESH,
        ).wait_recv()

    def wait_for(ref, size, sem, kinds):
        for kind in kinds:
            if KINDS[kind][0] < 2:
                arrived(ref, size, sem, kind)
        far = [kind for kind in kinds if KINDS[kind][0] == 2]
        if far:

            @pl.when(inner)
            def _():
                for kind in far:
                    arrived(ref, size, sem, kind)

    wait_for(meta_in, None, meta_recv_sem, range(1, 9))
    dec_geometry = geometry_weights(get(Arg.decode_geometry))
    for kind in range(9):
        rows = slice(kind * DEC, (kind + 1) * DEC)
        columns = meta_in[kind].T[0:DEC]
        group = pl.multiple_of(arrival_group(kind) * DEC, DEC)
        dec_onehot[rows, :] = column_onehot(columns[:, 0:1], NODES)
        dec_base[rows, :] = dot(
            column_onehot(dec_cols[pl.ds(group, DEC), 1:2], GRID), dec_table[...]
        ) + dot(columns[:, 8:24].astype(BF16), dec_geometry)
    lane = lax.broadcasted_iota(jnp.int32, (8, 128), 1)
    tiles = []
    for tile in range(3):
        placed = jnp.full((8, 128), -1.0, F32)
        for c in range(4 * tile, 4 * tile + 4):
            da, db, u, v = CELLS[c]
            slot = slot_of(da, db)
            low = 32 * (c % 4)
            shift = (low - 32 * (2 * u + v)) % 128
            chosen = meta_in[slot, 0:8, :]
            if shift:
                chosen = pltpu.roll(chosen, shift, 1)
            chosen = chosen + jnp.asarray((slot - 1) * NODES, jnp.int32).astype(F32)
            if da:
                chosen = jnp.where(reaches(da), chosen, -1.0)
            placed = jnp.where((lane >= low) & (lane < low + 32), chosen, placed)
        tiles.append(placed[2:3])
    border_onehot = row_onehot(jnp.concatenate(tiles, axis=1), 8 * NODES)
    for part in range(2):
        rows = slice(part * 256, (part + 1) * 256)
        far = column_onehot(
            proc_columns[HALF + part * 256 : HALF + (part + 1) * 256, 0:1] - float(NODES), 12 * HALO
        )
        comp[rows, :] = dot_last(far, border_onehot).astype(BF16)

    for kinds in ((0, 1, 2), (3, 4, 5), (6, 7, 8)):
        wait_for(enc_recv, ENC, enc_recv_sem, [kind for kind in kinds if kind])
        rows = slice(kinds[0] * ENC, (kinds[0] + 3) * ENC)
        pre = enc_recv[rows, :].astype(F32) + dot(enc_tgt_onehot[rows, :], enc_tgt_table[...])
        message = layer_norm(dot(silu(pre).astype(BF16), get(Arg.encode_output))).astype(BF16)
        for at, kind in enumerate(kinds):
            group = pl.multiple_of(arrival_group(kind) * ENC, ENC)
            msgs[pl.ds(group, ENC), :] = message[at * ENC : (at + 1) * ENC]
    enc_target_row = get_row(Arg.encode_targets)
    total = dot(row_onehot(enc_target_row, NODES), msgs[0 : 9 * ENC, :]).astype(BF16)
    hidden = silu(mesh_part[...] + dot(total, get(Arg.mesh_gather))).astype(BF16)
    mesh_one[...] = (mesh_rows.astype(F32) + layer_norm(dot(hidden, get(Arg.mesh_output)))).astype(BF16)

    def halo_copy(halo, source, kind, target, send_sem, recv_sem):
        return pltpu.make_async_remote_copy(
            src_ref=halo.at[pl.ds(source * NODES, NODES)],
            dst_ref=halo.at[pl.ds(target * NODES, NODES)],
            send_sem=send_sem.at[target],
            recv_sem=recv_sem.at[target],
            device_id=device(*place(kind)),
            device_id_type=MESH,
        )

    def spread(halo, send_sem, recv_sem):
        near = [halo_copy(halo, 0, kind, MIRROR[kind], send_sem, recv_sem) for kind in (3, 4, 1)]
        far = [halo_copy(halo, 0, kind, MIRROR[kind], send_sem, recv_sem) for kind in (7, 8, 2)]
        relays = [halo_copy(halo, kind, 1, kind + 2, send_sem, recv_sem) for kind in (3, 4)]
        near[0].start()
        near[1].start()

        @pl.when(inner)
        def _():
            for copy in far:
                copy.start()

        near[2].start()
        return near, far, relays

    def relay(halo, recv_sem, relays):
        for at, kind in enumerate((3, 4)):
            arrived(halo, NODES, recv_sem, kind)
            relays[at].start()

    halo_mesh[0:NODES, :] = dot(mesh_one[...], get(Arg.process_source)).astype(BF16)
    mesh_copies = spread(halo_mesh, mesh_send_sem, mesh_recv_sem)
    proc_tgt_table = dot(mesh_one[...], get(Arg.process_target)).astype(BF16)
    for part in range(4):
        rows = slice(part * 256, (part + 1) * 256)
        base[rows, :] = dot(proc_tgt_onehot[rows, :], proc_tgt_table) + dot(proc_geo[rows, :], proc_geometry)
        if part < 2:
            pre = base[rows, :] + dot(near_onehot[rows, :], halo_mesh[0:NODES, :])
            msgs[rows, :] = layer_norm(dot(silu(pre).astype(BF16), get(Arg.process_output))).astype(BF16)
    mesh_part[...] = dot(mesh_one[...], get(Arg.node_self))
    relay(halo_mesh, mesh_recv_sem, mesh_copies[2])
    wait_for(halo_mesh, NODES, mesh_recv_sem, (1, 2, 5, 6, 7, 8))
    for part in range(2, 4):
        rows = slice(part * 256, (part + 1) * 256)
        pre = base[rows, :] + dot(comp[(part - 2) * 256 : (part - 1) * 256, :], halo_mesh[NODES:, :])
        msgs[rows, :] = layer_norm(dot(silu(pre).astype(BF16), get(Arg.process_output))).astype(BF16)
    total = dot(row_onehot(proc_target_row, NODES), msgs[...]).astype(BF16)
    hidden = silu(mesh_part[...] + dot(total, get(Arg.node_gather))).astype(BF16)
    mesh_new = (mesh_one[...].astype(F32) + layer_norm(dot(hidden, get(Arg.node_output)))).astype(BF16)
    mesh_out[...] = mesh_new

    halo_back[0:NODES, :] = dot(mesh_new, get(Arg.decode_source)).astype(BF16)
    back_copies = spread(halo_back, back_send_sem, back_recv_sem)
    dec_scatter = row_onehot(get_row(Arg.decode_targets), GRID)
    for kinds in ((0, 1), (3, 4), (2, 5, 6), (7, 8)):
        if 3 in kinds:
            relay(halo_back, back_recv_sem, back_copies[2])
        else:
            wait_for(halo_back, NODES, back_recv_sem, [kind for kind in kinds if kind])
        hidden = []
        for kind in kinds:
            rows = slice(kind * DEC, (kind + 1) * DEC)
            pre = dec_base[rows, :] + dot(dec_onehot[rows, :], halo_back[kind * NODES : (kind + 1) * NODES, :])
            hidden.append(silu(pre).astype(BF16))
        message = layer_norm(dot(jnp.concatenate(hidden, axis=0), get(Arg.decode_output))).astype(BF16)
        for at, kind in enumerate(kinds):
            group = pl.multiple_of(arrival_group(kind) * DEC, DEC)
            msgs[pl.ds(group, DEC), :] = message[at * DEC : (at + 1) * DEC]
    total = dot(dec_scatter, msgs[0 : 9 * DEC, :]).astype(BF16)
    hidden = silu(grid_part[...] + dot(total, get(Arg.grid_gather))).astype(BF16)
    grid_out[...] = (refined[...].astype(F32) + layer_norm(dot(hidden, get(Arg.grid_output)))).astype(BF16)

    for g in OTHERS:
        da, db = OFFSETS[g]

        def sent(da=da, db=db, g=g):
            enc_copy(da, db, g).wait_send()
            meta_copy(da, db, g).wait_send()

        when(reaches(da), sent)
    for near, far, relays in (mesh_copies, back_copies):
        for copy in near + relays:
            copy.wait_send()

    @pl.when(inner)
    def _():
        for copies in (mesh_copies, back_copies):
            for copy in copies[1]:
                copy.wait_send()


def body(n_lat, n_lon, *arrays):
    dma = pltpu.SemaphoreType.DMA
    vmem = pltpu.VMEM
    scratch = [vmem(x.shape, x.dtype) for x in arrays]
    scratch += [dma((35,))] + [dma((9,)) for _ in range(8)]
    scratch += [
        vmem((24, 640), F32),
        vmem((640, 24), F32),
        vmem((24, EDGES), F32),
        vmem((24, 896), F32),
        vmem((896, 24), F32),
        vmem((9, 24, 128), F32),
        vmem((9, 24, 128), F32),
        vmem((9 * ENC, D), BF16),
        vmem((9 * ENC, D), BF16),
        vmem((GRID, D), BF16),
        vmem((NODES, D), BF16),
        vmem((9 * ENC, NODES), BF16),
        vmem((NODES, D), F32),
        vmem((GRID, D), F32),
        vmem((GRID, D), BF16),
        vmem((GRID, D), BF16),
        vmem((9 * DEC, D), F32),
        vmem((9 * DEC, NODES), BF16),
        vmem((HALF, 8 * NODES), BF16),
        vmem((EDGES, D), F32),
        vmem((HALF, NODES), BF16),
        vmem((EDGES, NODES), BF16),
        vmem((EDGES, 16), BF16),
        vmem((NODES, D), BF16),
        vmem((9 * NODES, D), BF16),
        vmem((9 * NODES, D), BF16),
        vmem((EDGES, D), BF16),
    ]
    return pl.pallas_call(
        functools.partial(kernel, n_lat, n_lon),
        out_shape=(
            jax.ShapeDtypeStruct((GRID, D), BF16),
            jax.ShapeDtypeStruct((NODES, D), BF16),
        ),
        in_specs=[pl.BlockSpec(memory_space=pl.ANY)] * 35,
        out_specs=[pl.BlockSpec(memory_space=pltpu.VMEM)] * 2,
        scratch_shapes=scratch,
        compiler_params=pltpu.CompilerParams(
            collective_id=0, has_side_effects=True, vmem_limit_bytes=40 * 2**20
        ),
        cost_estimate=pl.CostEstimate(flops=6 * 10**9, bytes_accessed=12 * 10**6, transcendentals=2 * 10**6),
    )(*[pltpu.with_memory_space_constraint(x, pltpu.HBM) for x in arrays])


def solution(mesh):
    n_lat, n_lon = mesh.shape["lat"], mesh.shape["lon"]
    rows = P(("lat", "lon"), None)
    line = P(("lat", "lon"))
    edges = P(None, ("lat", "lon"))
    placed = (rows, rows, line, line, edges, P("lat", "lon", None), line, line, edges, line, line, edges)
    placed += (P(),) * 23
    return jax.shard_map(
        functools.partial(body, n_lat, n_lon),
        mesh=mesh,
        in_specs=placed,
        out_specs=(rows, rows),
        check_vma=False,
    )
```

time: 45 us -> 40.5 us (0.900)
  the two profiles are of different devices: /device:TPU:0 before, /device:TPU:1 now
where the time goes in v3:
time: 40.5 us; the launch traced here: 40.3 us
  Pallas kernels  38.3 us (95%)
  local copies, waits for them, and re-layouts  1.33 us (3%)
  between operations  0.65 us (2%)
    pallas_call x1, Pallas kernels, body(): pl.pallas_call(functools.partial(kernel, n_lat, n_lon), out_shape=(jax.Sh...  38.3 us
    unnamed x2, local copies, waits for them, and re-layouts  1.33 us

profile of v3, /device:TPU:1, one launch (start us, length us, event | category | flops | bytes accessed | tf_op | source)
XLA Modules:
  0.0 40.3 jit_solution(17429161800060606120)
XLA Ops:
  0.6 38.3 %shard_map.338 = (bf16[256,512]{1,0:T(8,128)(2,1)S(1)}, bf16[64,512]{1,0:T(8,128)(2,1)S(1)}) custom-call(bf16[256,512]{1,0:T(8,128)(2,1)} %refs_0_.1, bf16[64,512]{1,0:T(8,128)(2,1)} %refs_1_.1, s32[576]{0:T(1024)} %refs_2_.1, s32[576]{0:T(1024)} %refs_3_.1, f32[4,576]{1,0:T(4,128)} %refs_4_.1, s32[2,2,32]{2,1,0:T(2,128)} %refs_5_.1, s32[1024]{0:T(1024)} %refs_6_.1, ...), custom_call_target="tpu_custom_call" | custom-call | flops 6000000000 | bytes 12000000 | tf_op jit(solution)/shard_map/pallas_call | solution.py:536
  39.0 0.7 %copy.39 = bf16[256,512]{1,0:T(8,128)(2,1)} copy(bf16[256,512]{1,0:T(8,128)(2,1)S(1)} %get-tuple-element.4) | data formatting | bytes 524288
  39.7 0.6 %copy.40 = bf16[64,512]{1,0:T(8,128)(2,1)} copy(bf16[64,512]{1,0:T(8,128)(2,1)S(1)} %get-tuple-element.5) | data formatting | bytes 131072

commit v4 on v3

--- a/solution.py
+++ b/solution.py
@@ -360,6 +360,61 @@
                 for kind in far:
                     arrived(ref, size, sem, kind)
 
+    for kinds in ((0, 1, 2), (3, 4, 5), (6, 7, 8)):
+        wait_for(enc_recv, ENC, enc_recv_sem, [kind for kind in kinds if kind])
+        rows = slice(kinds[0] * ENC, (kinds[0] + 3) * ENC)
+        pre = enc_recv[rows, :].astype(F32) + dot(enc_tgt_onehot[rows, :], enc_tgt_table[...])
+        message = layer_norm(dot(silu(pre).astype(BF16), get(Arg.encode_output))).astype(BF16)
+        for at, kind in enumerate(kinds):
+            group = pl.multiple_of(arrival_group(kind) * ENC, ENC)
+            msgs[pl.ds(group, ENC), :] = message[at * ENC : (at + 1) * ENC]
+    enc_target_row = get_row(Arg.encode_targets)
+    total = dot(row_onehot(enc_target_row, NODES), msgs[0 : 9 * ENC, :]).astype(BF16)
+    hidden = silu(mesh_part[...] + dot(total, get(Arg.mesh_gather))).astype(BF16)
+    mesh_one[...] = (mesh_rows.astype(F32) + layer_norm(dot(hidden, get(Arg.mesh_output)))).astype(BF16)
+
+    def halo_copy(halo, source, kind, target, send_sem, recv_sem):
+        return pltpu.make_async_remote_copy(
+            src_ref=halo.at[pl.ds(source * NODES, NODES)],
+            dst_ref=halo.at[pl.ds(target * NODES, NODES)],
+            send_sem=send_sem.at[target],
+            recv_sem=recv_sem.at[target],
+            device_id=device(*place(kind)),
+            device_id_type=MESH,
+        )
+
+    def spread(halo, send_sem, recv_sem):
+        near = [halo_copy(halo, 0, kind, MIRROR[kind], send_sem, recv_sem) for kind in (3, 4, 1)]
+        far = [halo_copy(halo, 0, kind, MIRROR[kind], send_sem, recv_sem) for kind in (7, 8, 2)]
+        relays = [halo_copy(halo, kind, 1, kind + 2, send_sem, recv_sem) for kind in (3, 4)]
+        near[0].start()
+        near[1].start()
+
+        @pl.when(inner)
+        def _():
+            for copy in far:
+                copy.start()
+
+        near[2].start()
+        return near, far, relays
+
+    def relay(halo, recv_sem, relays):
+        for at, kind in enumerate((3, 4)):
+            arrived(halo, NODES, recv_sem, kind)
+            relays[at].start()
+
+    halo_mesh[0:NODES, :] = dot(mesh_one[...], get(Arg.process_source)).astype(BF16)
+    mesh_copies = spread(halo_mesh, mesh_send_sem, mesh_recv_sem)
+    proc_tgt_table = dot(mesh_one[...], get(Arg.process_target)).astype(BF16)
+    for part in range(4):
+        rows = slice(part * 256, (part + 1) * 256)
+        base[rows, :] = dot(proc_tgt_onehot[rows, :], proc_tgt_table) + dot(proc_geo[rows, :], proc_geometry)
+        if part < 2:
+            pre = base[rows, :] + dot(near_onehot[rows, :], halo_mesh[0:NODES, :])
+            msgs[rows, :] = layer_norm(dot(silu(pre).astype(BF16), get(Arg.process_output))).astype(BF16)
+    mesh_part[...] = dot(mesh_one[...], get(Arg.node_self))
+    near_total = dot(row_onehot(proc_target_row[:, 0:HALF], NODES), msgs[0:HALF, :])
+
     wait_for(meta_in, None, meta_recv_sem, range(1, 9))
     dec_geometry = geometry_weights(get(Arg.decode_geometry))
     for kind in range(9):
@@ -395,66 +450,13 @@
         )
         comp[rows, :] = dot_last(far, border_onehot).astype(BF16)
 
-    for kinds in ((0, 1, 2), (3, 4, 5), (6, 7, 8)):
-        wait_for(enc_recv, ENC, enc_recv_sem, [kind for kind in kinds if kind])
-        rows = slice(kinds[0] * ENC, (kinds[0] + 3) * ENC)
-        pre = enc_recv[rows, :].astype(F32) + dot(enc_tgt_onehot[rows, :], enc_tgt_table[...])
-        message = layer_norm(dot(silu(pre).astype(BF16), get(Arg.encode_output))).astype(BF16)
-        for at, kind in enumerate(kinds):
-            group = pl.multiple_of(arrival_group(kind) * ENC, ENC)
-            msgs[pl.ds(group, ENC), :] = message[at * ENC : (at + 1) * ENC]
-    enc_target_row = get_row(Arg.encode_targets)
-    total = dot(row_onehot(enc_target_row, NODES), msgs[0 : 9 * ENC, :]).astype(BF16)
-    hidden = silu(mesh_part[...] + dot(total, get(Arg.mesh_gather))).astype(BF16)
-    mesh_one[...] = (mesh_rows.astype(F32) + layer_norm(dot(hidden, get(Arg.mesh_output)))).astype(BF16)
-
-    def halo_copy(halo, source, kind, target, send_sem, recv_sem):
-        return pltpu.make_async_remote_copy(
-            src_ref=halo.at[pl.ds(source * NODES, NODES)],
-            dst_ref=halo.at[pl.ds(target * NODES, NODES)],
-            send_sem=send_sem.at[target],
-            recv_sem=recv_sem.at[target],
-            device_id=device(*place(kind)),
-            device_id_type=MESH,
-        )
-
-    def spread(halo, send_sem, recv_sem):
-        near = [halo_copy(halo, 0, kind, MIRROR[kind], send_sem, recv_sem) for kind in (3, 4, 1)]
-        far = [halo_copy(halo, 0, kind, MIRROR[kind], send_sem, recv_sem) for kind in (7, 8, 2)]
-        relays = [halo_copy(halo, kind, 1, kind + 2, send_sem, recv_sem) for kind in (3, 4)]
-        near[0].start()
-        near[1].start()
-
-        @pl.when(inner)
-        def _():
-            for copy in far:
-                copy.start()
-
-        near[2].start()
-        return near, far, relays
-
-    def relay(halo, recv_sem, relays):
-        for at, kind in enumerate((3, 4)):
-            arrived(halo, NODES, recv_sem, kind)
-            relays[at].start()
-
-    halo_mesh[0:NODES, :] = dot(mesh_one[...], get(Arg.process_source)).astype(BF16)
-    mesh_copies = spread(halo_mesh, mesh_send_sem, mesh_recv_sem)
-    proc_tgt_table = dot(mesh_one[...], get(Arg.process_target)).astype(BF16)
-    for part in range(4):
-        rows = slice(part * 256, (part + 1) * 256)
-        base[rows, :] = dot(proc_tgt_onehot[rows, :], proc_tgt_table) + dot(proc_geo[rows, :], proc_geometry)
-        if part < 2:
-            pre = base[rows, :] + dot(near_onehot[rows, :], halo_mesh[0:NODES, :])
-            msgs[rows, :] = layer_norm(dot(silu(pre).astype(BF16), get(Arg.process_output))).astype(BF16)
-    mesh_part[...] = dot(mesh_one[...], get(Arg.node_self))
     relay(halo_mesh, mesh_recv_sem, mesh_copies[2])
     wait_for(halo_mesh, NODES, mesh_recv_sem, (1, 2, 5, 6, 7, 8))
     for part in range(2, 4):
         rows = slice(part * 256, (part + 1) * 256)
         pre = base[rows, :] + dot(comp[(part - 2) * 256 : (part - 1) * 256, :], halo_mesh[NODES:, :])
         msgs[rows, :] = layer_norm(dot(silu(pre).astype(BF16), get(Arg.process_output))).astype(BF16)
-    total = dot(row_onehot(proc_target_row, NODES), msgs[...]).astype(BF16)
+    total = (near_total + dot(row_onehot(proc_target_row[:, HALF:], NODES), msgs[HALF:, :])).astype(BF16)
     hidden = silu(mesh_part[...] + dot(total, get(Arg.node_gather))).astype(BF16)
     mesh_new = (mesh_one[...].astype(F32) + layer_norm(dot(hidden, get(Arg.node_output)))).astype(BF16)
     mesh_out[...] = mesh_new

time: 40.5 us -> 35.5 us (0.88)
  Pallas kernels: 38.3 us -> 33.3 us
    pallas_call x1, Pallas kernels: 38.3 us -> 33.3 us  [body(): pl.pallas_call(functools.partial(kernel, n_lat, n_lon), out_shape=(jax.Sh...]
where the time goes in v4:
time: 35.5 us; the launch traced here: 35.3 us
  Pallas kernels  33.3 us (94%)
  local copies, waits for them, and re-layouts  1.33 us (4%)
  between operations  0.65 us (2%)
    pallas_call x1, Pallas kernels, body(): pl.pallas_call(functools.partial(kernel, n_lat, n_lon), out_shape=(jax.Sh...  33.3 us
    unnamed x2, local copies, waits for them, and re-layouts  1.33 us

profile of v4, /device:TPU:1, one launch (start us, length us, event | category | flops | bytes accessed | tf_op | source)
XLA Modules:
  0.0 35.3 jit_solution(7805410877005881605)
XLA Ops:
  0.6 33.3 %shard_map.338 = (bf16[256,512]{1,0:T(8,128)(2,1)S(1)}, bf16[64,512]{1,0:T(8,128)(2,1)S(1)}) custom-call(bf16[256,512]{1,0:T(8,128)(2,1)} %refs_0_.1, bf16[64,512]{1,0:T(8,128)(2,1)} %refs_1_.1, s32[576]{0:T(1024)} %refs_2_.1, s32[576]{0:T(1024)} %refs_3_.1, f32[4,576]{1,0:T(4,128)} %refs_4_.1, s32[2,2,32]{2,1,0:T(2,128)} %refs_5_.1, s32[1024]{0:T(1024)} %refs_6_.1, ...), custom_call_target="tpu_custom_call" | custom-call | flops 6000000000 | bytes 12000000 | tf_op jit(solution)/shard_map/pallas_call | solution.py:538
  34.0 0.7 %copy.39 = bf16[256,512]{1,0:T(8,128)(2,1)} copy(bf16[256,512]{1,0:T(8,128)(2,1)S(1)} %get-tuple-element.4) | data formatting | bytes 524288
  34.7 0.6 %copy.40 = bf16[64,512]{1,0:T(8,128)(2,1)} copy(bf16[64,512]{1,0:T(8,128)(2,1)S(1)} %get-tuple-element.5) | data formatting | bytes 131072

commit v5 on v4

--- a/solution.py
+++ b/solution.py
@@ -19,6 +19,8 @@
 DEC = 96
 EDGES = 1024
 HALF = EDGES // 2
+EARLY = 640
+CORNERS = 7 * NODES
 OFFSETS = [(g // 3 - 1, g % 3 - 1) for g in range(9)]
 OTHERS = [g for g in range(9) if g != 4]
 CELLS = [
@@ -130,6 +132,11 @@
     return centred * lax.rsqrt(variance + 1e-05)
 
 
+def norm_centred(values):
+    variance = jnp.mean(values * values, axis=-1, keepdims=True)
+    return values * lax.rsqrt(variance + 1e-05)
+
+
 def column_onehot(column, width):
     lanes = lax.broadcasted_iota(jnp.int32, (column.shape[0], width), 1).astype(F32)
     return jnp.where(column == lanes, 1.0, 0.0).astype(BF16)
@@ -162,7 +169,7 @@
     (
         load_sem, enc_send_sem, enc_recv_sem, meta_send_sem, meta_recv_sem,
         mesh_send_sem, mesh_recv_sem, back_send_sem, back_recv_sem,
-        enc_rows, enc_cols, proc_rows, dec_rows, dec_cols, meta_out, meta_in,
+        enc_rows, proc_rows, dec_rows, corner_cols, corner_onehot, corner, meta_out, meta_in,
         enc_send, enc_recv, enc_table, enc_tgt_table, enc_tgt_onehot,
         mesh_part, grid_part, refined, dec_table, dec_base, dec_onehot,
         comp, base, near_onehot, proc_tgt_onehot, proc_geo,
@@ -214,6 +221,12 @@
     def get_row(name):
         return get(name).reshape(1, -1).astype(F32)
 
+    def centre(name):
+        get(name)
+        for at in range(0, D, 128):
+            weights = vmem[name][at : at + 128, :].astype(F32)
+            vmem[name][at : at + 128, :] = (weights - jnp.mean(weights, axis=-1, keepdims=True)).astype(BF16)
+
     load(FIRST)
     barrier = pltpu.get_barrier_semaphore()
     for g in OTHERS:
@@ -230,20 +243,20 @@
         for kind in range(9):
             if KINDS[kind][0] == 2:
                 enc_recv[kind * ENC : (kind + 1) * ENC, :] = jnp.zeros((ENC, D), BF16)
-                halo_mesh[kind * NODES : (kind + 1) * NODES, :] = jnp.zeros((NODES, D), BF16)
+                if kind == 2:
+                    halo_mesh[kind * NODES : (kind + 1) * NODES, :] = jnp.zeros((NODES, D), BF16)
                 halo_back[kind * NODES : (kind + 1) * NODES, :] = jnp.zeros((NODES, D), BF16)
                 meta_in[kind] = jnp.zeros((24, 128), F32)
+        halo_mesh[CORNERS:, :] = jnp.zeros((2 * HALO, D), BF16)
 
     enc_rows[...] = jnp.zeros_like(enc_rows)
     enc_rows[0:1, 0 : 9 * ENC] = get_row(Arg.encode_sources)
     enc_rows[1:2, 0 : 9 * ENC] = get_row(Arg.encode_targets)
     enc_rows[8:24, 0 : 9 * ENC] = geometry_rows(get(Arg.encode_edges))
     enc_columns = enc_rows[...].T
-    enc_cols[...] = enc_columns
     enc_geometry = geometry_weights(get(Arg.encode_geometry))
     enc_table[...] = dot(get(Arg.grid_in), get(Arg.encode_source)).astype(BF16)
     load(THIRD)
-    slots = []
     for part in range(3):
         rows = slice(part * 3 * ENC, (part + 1) * 3 * ENC)
         columns = enc_columns[rows]
@@ -310,7 +323,10 @@
             meta_copy(da, db, g).start()
 
         when(reaches(da), send_meta)
-    dec_cols[...] = dec_all.T
+
+    corner_cols[...] = meta_out[4].T
+    corner_rows = pl.ds(pl.multiple_of(jnp.where(even, 0, 2 * HALO), 2 * HALO), 2 * HALO)
+    corner_onehot[...] = column_onehot(corner_cols[corner_rows, 2:3], NODES)
 
     grid_rows = get(Arg.grid_in)
     hidden = silu(dot(grid_rows, get(Arg.refine_hidden))).astype(BF16)
@@ -320,12 +336,6 @@
     mesh_rows = get(Arg.mesh_in)
     enc_tgt_table[...] = dot(mesh_rows, get(Arg.encode_target)).astype(BF16)
     mesh_part[...] = dot(mesh_rows, get(Arg.mesh_self))
-    for kind in range(9):
-        group = pl.multiple_of(arrival_group(kind) * ENC, ENC)
-        enc_tgt_onehot[kind * ENC : (kind + 1) * ENC, :] = column_onehot(
-            enc_cols[pl.ds(group, ENC), 1:2], NODES
-        )
-
     proc_rows[...] = jnp.zeros_like(proc_rows)
     proc_rows[0:1, :] = get_row(Arg.process_sources)
     proc_target_row = get_row(Arg.process_targets)
@@ -337,16 +347,38 @@
     proc_geo[...] = proc_columns[:, 8:24].astype(BF16)
     proc_geometry = geometry_weights(get(Arg.process_geometry))
 
+    def block(halo, kind):
+        if halo is halo_mesh and kind > 6:
+            return halo.at[pl.ds(CORNERS + (kind - 7) * HALO, HALO)]
+        return halo.at[pl.ds(kind * NODES, NODES)]
+
     def arrived(ref, size, sem, kind):
-        block = ref.at[kind] if size is None else ref.at[pl.ds(kind * size, size)]
+        if ref is halo_mesh:
+            landed = block(ref, kind)
+        else:
+            landed = ref.at[kind] if size is None else ref.at[pl.ds(kind * size, size)]
         pltpu.make_async_remote_copy(
-            src_ref=block,
-            dst_ref=block,
+            src_ref=landed,
+            dst_ref=landed,
             send_sem=enc_send_sem.at[kind],
             recv_sem=sem.at[kind],
             device_id=device(*place(1)),
             device_id_type=MESH,
         ).wait_recv()
+
+    def by_kind(rows, size):
+        lanes = lax.broadcasted_iota(jnp.int32, rows.shape, 1)
+        width = rows.shape[1]
+        placed = rows
+        for kind in range(9):
+            vertical, db = KINDS[kind]
+            moved = []
+            for da in ((0,) if vertical == 0 else ((1, -1) if vertical == 1 else (-1, 1))):
+                shift = ((kind - ((1 - da) * 3 + (1 - db))) * size) % width
+                moved.append(pltpu.roll(rows, shift, 1) if shift else rows)
+            block = moved[0] if vertical == 0 else jnp.where(even, moved[0], moved[1])
+            placed = jnp.where((lanes >= kind * size) & (lanes < (kind + 1) * size), block, placed)
+        return placed
 
     def wait_for(ref, size, sem, kinds):
         for kind in kinds:
@@ -360,23 +392,29 @@
                 for kind in far:
                     arrived(ref, size, sem, kind)
 
-    for kinds in ((0, 1, 2), (3, 4, 5), (6, 7, 8)):
+    enc_targets = by_kind(enc_rows[0:8, :], ENC)
+    enc_tgt_onehot[...] = column_onehot(enc_targets.T[0 : 9 * ENC, 1:2], NODES)
+    enc_scatter = row_onehot(enc_targets[1:2], NODES)
+    for name in (Arg.encode_output, Arg.mesh_output, Arg.process_output, Arg.node_output):
+        centre(name)
+    for name in list(loads):
+        get(name)
+
+    total = jnp.zeros((NODES, D), F32)
+    for kinds in ((0, 1), (2, 3, 4, 5), (6, 7, 8)):
         wait_for(enc_recv, ENC, enc_recv_sem, [kind for kind in kinds if kind])
-        rows = slice(kinds[0] * ENC, (kinds[0] + 3) * ENC)
+        rows = slice(kinds[0] * ENC, (kinds[-1] + 1) * ENC)
         pre = enc_recv[rows, :].astype(F32) + dot(enc_tgt_onehot[rows, :], enc_tgt_table[...])
-        message = layer_norm(dot(silu(pre).astype(BF16), get(Arg.encode_output))).astype(BF16)
-        for at, kind in enumerate(kinds):
-            group = pl.multiple_of(arrival_group(kind) * ENC, ENC)
-            msgs[pl.ds(group, ENC), :] = message[at * ENC : (at + 1) * ENC]
-    enc_target_row = get_row(Arg.encode_targets)
-    total = dot(row_onehot(enc_target_row, NODES), msgs[0 : 9 * ENC, :]).astype(BF16)
+        message = norm_centred(dot(silu(pre).astype(BF16), get(Arg.encode_output))).astype(BF16)
+        total = total + dot(enc_scatter[:, rows], message)
+    total = total.astype(BF16)
     hidden = silu(mesh_part[...] + dot(total, get(Arg.mesh_gather))).astype(BF16)
-    mesh_one[...] = (mesh_rows.astype(F32) + layer_norm(dot(hidden, get(Arg.mesh_output)))).astype(BF16)
+    mesh_one[...] = (mesh_rows.astype(F32) + norm_centred(dot(hidden, get(Arg.mesh_output)))).astype(BF16)
 
     def halo_copy(halo, source, kind, target, send_sem, recv_sem):
         return pltpu.make_async_remote_copy(
-            src_ref=halo.at[pl.ds(source * NODES, NODES)],
-            dst_ref=halo.at[pl.ds(target * NODES, NODES)],
+            src_ref=source,
+            dst_ref=block(halo, target),
             send_sem=send_sem.at[target],
             recv_sem=recv_sem.at[target],
             device_id=device(*place(kind)),
@@ -384,11 +422,19 @@
         )
 
     def spread(halo, send_sem, recv_sem):
-        near = [halo_copy(halo, 0, kind, MIRROR[kind], send_sem, recv_sem) for kind in (3, 4, 1)]
-        far = [halo_copy(halo, 0, kind, MIRROR[kind], send_sem, recv_sem) for kind in (7, 8, 2)]
-        relays = [halo_copy(halo, kind, 1, kind + 2, send_sem, recv_sem) for kind in (3, 4)]
+        own = block(halo, 0)
+        near = [halo_copy(halo, own, kind, MIRROR[kind], send_sem, recv_sem) for kind in (3, 4, 1)]
+        relays = [halo_copy(halo, block(halo, kind), 1, kind + 2, send_sem, recv_sem) for kind in (3, 4)]
         near[0].start()
         near[1].start()
+        sources = [own, own]
+        if halo is halo_mesh:
+            corner[...] = dot(corner_onehot[...], halo[0:NODES, :]).astype(BF16)
+            sources = [corner.at[pl.ds(HALO, HALO)], corner.at[pl.ds(0, HALO)]]
+        far = [
+            halo_copy(halo, source, kind, MIRROR[kind], send_sem, recv_sem)
+            for kind, source in zip((7, 8, 2), sources + [own])
+        ]
 
         @pl.when(inner)
         def _():
@@ -397,6 +443,16 @@
 
         near[2].start()
         return near, far, relays
+
+    def sent_all(copies):
+        near, far, relays = copies
+        for copy in near + relays:
+            copy.wait_send()
+
+        @pl.when(inner)
+        def _():
+            for copy in far:
+                copy.wait_send()
 
     def relay(halo, recv_sem, relays):
         for at, kind in enumerate((3, 4)):
@@ -411,19 +467,22 @@
         base[rows, :] = dot(proc_tgt_onehot[rows, :], proc_tgt_table) + dot(proc_geo[rows, :], proc_geometry)
         if part < 2:
             pre = base[rows, :] + dot(near_onehot[rows, :], halo_mesh[0:NODES, :])
-            msgs[rows, :] = layer_norm(dot(silu(pre).astype(BF16), get(Arg.process_output))).astype(BF16)
+            msgs[rows, :] = norm_centred(dot(silu(pre).astype(BF16), get(Arg.process_output))).astype(BF16)
     mesh_part[...] = dot(mesh_one[...], get(Arg.node_self))
     near_total = dot(row_onehot(proc_target_row[:, 0:HALF], NODES), msgs[0:HALF, :])
 
     wait_for(meta_in, None, meta_recv_sem, range(1, 9))
+    dec_targets = by_kind(dec_rows[0:8, :], DEC)
+    dec_columns = dec_targets.T
     dec_geometry = geometry_weights(get(Arg.decode_geometry))
+    for name in (Arg.decode_output, Arg.grid_output):
+        centre(name)
     for kind in range(9):
         rows = slice(kind * DEC, (kind + 1) * DEC)
         columns = meta_in[kind].T[0:DEC]
-        group = pl.multiple_of(arrival_group(kind) * DEC, DEC)
         dec_onehot[rows, :] = column_onehot(columns[:, 0:1], NODES)
         dec_base[rows, :] = dot(
-            column_onehot(dec_cols[pl.ds(group, DEC), 1:2], GRID), dec_table[...]
+            column_onehot(dec_columns[rows, 1:2], GRID), dec_table[...]
         ) + dot(columns[:, 8:24].astype(BF16), dec_geometry)
     lane = lax.broadcasted_iota(jnp.int32, (8, 128), 1)
     tiles = []
@@ -434,15 +493,18 @@
             slot = slot_of(da, db)
             low = 32 * (c % 4)
             shift = (low - 32 * (2 * u + v)) % 128
+            corner_row = CORNERS - NODES + (0 if db == 1 else HALO) - low
             chosen = meta_in[slot, 0:8, :]
             if shift:
                 chosen = pltpu.roll(chosen, shift, 1)
             chosen = chosen + jnp.asarray((slot - 1) * NODES, jnp.int32).astype(F32)
+            if da and db:
+                chosen = jnp.where(steps[1] == da, chosen, (lane + corner_row).astype(F32))
             if da:
                 chosen = jnp.where(reaches(da), chosen, -1.0)
             placed = jnp.where((lane >= low) & (lane < low + 32), chosen, placed)
         tiles.append(placed[2:3])
-    border_onehot = row_onehot(jnp.concatenate(tiles, axis=1), 8 * NODES)
+    border_onehot = row_onehot(jnp.concatenate(tiles, axis=1), CORNERS)
     for part in range(2):
         rows = slice(part * 256, (part + 1) * 256)
         far = column_onehot(
@@ -450,22 +512,31 @@
         )
         comp[rows, :] = dot_last(far, border_onehot).astype(BF16)
 
+    for g in OTHERS:
+        da, db = OFFSETS[g]
+
+        def sent(da=da, db=db, g=g):
+            enc_copy(da, db, g).wait_send()
+            meta_copy(da, db, g).wait_send()
+
+        when(reaches(da), sent)
     relay(halo_mesh, mesh_recv_sem, mesh_copies[2])
     wait_for(halo_mesh, NODES, mesh_recv_sem, (1, 2, 5, 6, 7, 8))
     for part in range(2, 4):
         rows = slice(part * 256, (part + 1) * 256)
         pre = base[rows, :] + dot(comp[(part - 2) * 256 : (part - 1) * 256, :], halo_mesh[NODES:, :])
-        msgs[rows, :] = layer_norm(dot(silu(pre).astype(BF16), get(Arg.process_output))).astype(BF16)
+        msgs[rows, :] = norm_centred(dot(silu(pre).astype(BF16), get(Arg.process_output))).astype(BF16)
     total = (near_total + dot(row_onehot(proc_target_row[:, HALF:], NODES), msgs[HALF:, :])).astype(BF16)
     hidden = silu(mesh_part[...] + dot(total, get(Arg.node_gather))).astype(BF16)
-    mesh_new = (mesh_one[...].astype(F32) + layer_norm(dot(hidden, get(Arg.node_output)))).astype(BF16)
+    mesh_new = (mesh_one[...].astype(F32) + norm_centred(dot(hidden, get(Arg.node_output)))).astype(BF16)
     mesh_out[...] = mesh_new
 
     halo_back[0:NODES, :] = dot(mesh_new, get(Arg.decode_source)).astype(BF16)
     back_copies = spread(halo_back, back_send_sem, back_recv_sem)
-    dec_scatter = row_onehot(get_row(Arg.decode_targets), GRID)
+    dec_scatter = row_onehot(dec_targets[1:2, 0 : 9 * DEC], GRID)
     for kinds in ((0, 1), (3, 4), (2, 5, 6), (7, 8)):
         if 3 in kinds:
+            sent_all(mesh_copies)
             relay(halo_back, back_recv_sem, back_copies[2])
         else:
             wait_for(halo_back, NODES, back_recv_sem, [kind for kind in kinds if kind])
@@ -474,31 +545,38 @@
             rows = slice(kind * DEC, (kind + 1) * DEC)
             pre = dec_base[rows, :] + dot(dec_onehot[rows, :], halo_back[kind * NODES : (kind + 1) * NODES, :])
             hidden.append(silu(pre).astype(BF16))
-        message = layer_norm(dot(jnp.concatenate(hidden, axis=0), get(Arg.decode_output))).astype(BF16)
+        message = norm_centred(dot(jnp.concatenate(hidden, axis=0), get(Arg.decode_output))).astype(BF16)
         for at, kind in enumerate(kinds):
-            group = pl.multiple_of(arrival_group(kind) * DEC, DEC)
-            msgs[pl.ds(group, DEC), :] = message[at * DEC : (at + 1) * DEC]
-    total = dot(dec_scatter, msgs[0 : 9 * DEC, :]).astype(BF16)
+            msgs[kind * DEC : (kind + 1) * DEC, :] = message[at * DEC : (at + 1) * DEC]
+        if 6 in kinds:
+            early = dot(dec_scatter[:, 0:EARLY], msgs[0:EARLY, :])
+    total = (early + dot(dec_scatter[:, EARLY:], msgs[EARLY : 9 * DEC, :])).astype(BF16)
     hidden = silu(grid_part[...] + dot(total, get(Arg.grid_gather))).astype(BF16)
-    grid_out[...] = (refined[...].astype(F32) + layer_norm(dot(hidden, get(Arg.grid_output)))).astype(BF16)
-
-    for g in OTHERS:
-        da, db = OFFSETS[g]
-
-        def sent(da=da, db=db, g=g):
-            enc_copy(da, db, g).wait_send()
-            meta_copy(da, db, g).wait_send()
-
-        when(reaches(da), sent)
-    for near, far, relays in (mesh_copies, back_copies):
-        for copy in near + relays:
-            copy.wait_send()
-
-    @pl.when(inner)
-    def _():
-        for copies in (mesh_copies, back_copies):
-            for copy in copies[1]:
-                copy.wait_send()
+    grid_out[...] = (refined[...].astype(F32) + norm_centred(dot(hidden, get(Arg.grid_output)))).astype(BF16)
+
+    sent_all(back_copies)
+
+
+def hand_over_kernel(grid_ref, mesh_ref, grid_out, mesh_out, sems):
+    copies = [
+        pltpu.make_async_copy(grid_ref, grid_out, sems.at[0]),
+        pltpu.make_async_copy(mesh_ref, mesh_out, sems.at[1]),
+    ]
+    for copy in copies:
+        copy.start()
+    for copy in copies:
+        copy.wait()
+
+
+def hand_over(grid, mesh):
+    return pl.pallas_call(
+        hand_over_kernel,
+        out_shape=tuple(jax.ShapeDtypeStruct(x.shape, x.dtype) for x in (grid, mesh)),
+        in_specs=[pl.BlockSpec(memory_space=pl.ANY)] * 2,
+        out_specs=[pl.BlockSpec(memory_space=pl.ANY)] * 2,
+        scratch_shapes=[pltpu.SemaphoreType.DMA((2,))],
+        compiler_params=pltpu.CompilerParams(vmem_limit_bytes=8 * 2**20),
+    )(grid, mesh)
 
 
 def body(n_lat, n_lon, *arrays):
@@ -508,10 +586,11 @@
     scratch += [dma((35,))] + [dma((9,)) for _ in range(8)]
     scratch += [
         vmem((24, 640), F32),
-        vmem((640, 24), F32),
         vmem((24, EDGES), F32),
         vmem((24, 896), F32),
-        vmem((896, 24), F32),
+        vmem((128, 24), F32),
+        vmem((NODES, NODES), BF16),
+        vmem((2 * HALO, D), BF16),
         vmem((9, 24, 128), F32),
         vmem((9, 24, 128), F32),
         vmem((9 * ENC, D), BF16),
@@ -525,17 +604,17 @@
         vmem((GRID, D), BF16),
         vmem((9 * DEC, D), F32),
         vmem((9 * DEC, NODES), BF16),
-        vmem((HALF, 8 * NODES), BF16),
+        vmem((HALF, CORNERS), BF16),
         vmem((EDGES, D), F32),
         vmem((HALF, NODES), BF16),
         vmem((EDGES, NODES), BF16),
         vmem((EDGES, 16), BF16),
         vmem((NODES, D), BF16),
-        vmem((9 * NODES, D), BF16),
+        vmem((8 * NODES, D), BF16),
         vmem((9 * NODES, D), BF16),
         vmem((EDGES, D), BF16),
     ]
-    return pl.pallas_call(
+    grid, mesh = pl.pallas_call(
         functools.partial(kernel, n_lat, n_lon),
         out_shape=(
             jax.ShapeDtypeStruct((GRID, D), BF16),
@@ -549,6 +628,7 @@
         ),
         cost_estimate=pl.CostEstimate(flops=6 * 10**9, bytes_accessed=12 * 10**6, transcendentals=2 * 10**6),
     )(*[pltpu.with_memory_space_constraint(x, pltpu.HBM) for x in arrays])
+    return hand_over(grid, mesh)
 
 
 def solution(mesh):

time: 35.5 us -> 34.3 us (0.966)
  local copies, waits for them, and re-layouts: 1.33 us -> 0 us
    unnamed x2 -> x0, local copies, waits for them, and re-layouts: 1.33 us -> none
    pallas_call x0 -> x1, Pallas kernels: none -> 0.74 us  [hand_over(): pl.pallas_call(hand_over_kernel, out_shape=tuple((jax.ShapeDtypeStruct(x....]
    pallas_call x1, Pallas kernels: 33.3 us -> 32.8 us  [body(): pl.pallas_call(functools.partial(kernel, n_lat, n_lon), out_shape=(jax.Sh...]
where the time goes in v5:
time: 34.3 us; the launch traced here: 34.2 us
  Pallas kernels  33.6 us (98%)
  between operations  0.65 us (2%)
    pallas_call x1, Pallas kernels, body(): pl.pallas_call(functools.partial(kernel, n_lat, n_lon), out_shape=(jax.Sh...  32.8 us
    pallas_call x1, Pallas kernels, hand_over(): pl.pallas_call(hand_over_kernel, out_shape=tuple((jax.ShapeDtypeStruct(x....  0.74 us

profile of v5, /device:TPU:1, one launch (start us, length us, event | category | flops | bytes accessed | tf_op | source)
XLA Modules:
  0.0 34.2 jit_solution(12964103437115227970)
XLA Ops:
  0.6 32.8 %shard_map.338 = (bf16[256,512]{1,0:T(8,128)(2,1)S(1)}, bf16[64,512]{1,0:T(8,128)(2,1)S(1)}) custom-call(bf16[256,512]{1,0:T(8,128)(2,1)} %refs_0_.1, bf16[64,512]{1,0:T(8,128)(2,1)} %refs_1_.1, s32[576]{0:T(1024)} %refs_2_.1, s32[576]{0:T(1024)} %refs_3_.1, f32[4,576]{1,0:T(4,128)} %refs_4_.1, s32[2,2,32]{2,1,0:T(2,128)} %refs_5_.1, s32[1024]{0:T(1024)} %refs_6_.1, ...), custom_call_target="tpu_custom_call" | custom-call | flops 6000000000 | bytes 12000000 | tf_op jit(solution)/shard_map/pallas_call | solution.py:617
  33.5 0.7 %shard_map.339 = (bf16[256,512]{1,0:T(8,128)(2,1)}, bf16[64,512]{1,0:T(8,128)(2,1)}) custom-call(bf16[256,512]{1,0:T(8,128)(2,1)S(1)} %get-tuple-element.4.grid_ref, bf16[64,512]{1,0:T(8,128)(2,1)S(1)} %get-tuple-element.5.mesh_ref), custom_call_target="tpu_custom_call" | custom-call | tf_op jit(solution)/shard_map/pallas_call | solution.py:572

commit v6 on v5

--- a/solution.py
+++ b/solution.py
@@ -168,8 +168,8 @@
     vmem = dict(zip(Arg, refs[37:72]))
     (
         load_sem, enc_send_sem, enc_recv_sem, meta_send_sem, meta_recv_sem,
-        mesh_send_sem, mesh_recv_sem, back_send_sem, back_recv_sem,
-        enc_rows, proc_rows, dec_rows, corner_cols, corner_onehot, corner, meta_out, meta_in,
+        mesh_send_sem, mesh_recv_sem,
+        enc_rows, enc_cols, proc_rows, dec_rows, corner_cols, corner_onehot, corner, meta_out, meta_in,
         enc_send, enc_recv, enc_table, enc_tgt_table, enc_tgt_onehot,
         mesh_part, grid_part, refined, dec_table, dec_base, dec_onehot,
         comp, base, near_onehot, proc_tgt_onehot, proc_geo,
@@ -188,10 +188,6 @@
         vertical, db = KINDS[kind]
         return steps[vertical], db
 
-    def arrival_group(kind):
-        da, db = place(kind)
-        return (1 - da) * 3 + (1 - db)
-
     def slot_of(da, db):
         if da == 0:
             return KINDS.index((0, db))
@@ -253,42 +249,43 @@
     enc_rows[0:1, 0 : 9 * ENC] = get_row(Arg.encode_sources)
     enc_rows[1:2, 0 : 9 * ENC] = get_row(Arg.encode_targets)
     enc_rows[8:24, 0 : 9 * ENC] = geometry_rows(get(Arg.encode_edges))
-    enc_columns = enc_rows[...].T
+    enc_cols[...] = enc_rows[...].T
     enc_geometry = geometry_weights(get(Arg.encode_geometry))
+
+    def enc_columns(vertical):
+        first = pl.multiple_of((steps[vertical] + 1) * 3 * ENC, 3 * ENC)
+        columns = enc_cols[pl.ds(first, 3 * ENC), :]
+        return column_onehot(columns[:, 0:1], GRID), dot(columns[:, 8:24].astype(BF16), enc_geometry)
+
+    def enc_copy(kind):
+        vertical, db = KINDS[kind]
+        return pltpu.make_async_remote_copy(
+            src_ref=enc_send.at[pl.ds((3 * vertical + db + 1) * ENC, ENC)],
+            dst_ref=enc_recv.at[pl.ds(MIRROR[kind] * ENC, ENC)],
+            send_sem=enc_send_sem.at[kind],
+            recv_sem=enc_recv_sem.at[MIRROR[kind]],
+            device_id=device(*place(kind)),
+            device_id_type=MESH,
+        )
+
+    onehot, geometry = enc_columns(2)
     enc_table[...] = dot(get(Arg.grid_in), get(Arg.encode_source)).astype(BF16)
+    enc_send[6 * ENC : 9 * ENC, :] = (dot(onehot, enc_table[...]) + geometry).astype(BF16)
     load(THIRD)
-    for part in range(3):
-        rows = slice(part * 3 * ENC, (part + 1) * 3 * ENC)
-        columns = enc_columns[rows]
-        enc_send[rows, :] = (
-            dot(column_onehot(columns[:, 0:1], GRID), enc_table[...])
-            + dot(columns[:, 8:24].astype(BF16), enc_geometry)
-        ).astype(BF16)
-        if part == 0:
-            pl.semaphore_wait(barrier, jnp.where(inner, 8, 5))
-        for g in range(3 * part, 3 * part + 3):
-            if g == 4:
-                enc_recv[0:ENC, :] = enc_send[g * ENC : (g + 1) * ENC, :]
-                continue
-            da, db = OFFSETS[g]
-
-            def send(da=da, db=db, g=g):
-                enc_copy(da, db, g).start()
-
-            def enc_copy(da, db, g):
-                slot = slot_of(-da, -db) if da == 0 else jnp.where(
-                    steps[1] == da, KINDS.index((1, -db)), KINDS.index((2, -db))
-                )
-                return pltpu.make_async_remote_copy(
-                    src_ref=enc_send.at[pl.ds(g * ENC, ENC)],
-                    dst_ref=enc_recv.at[pl.ds(pl.multiple_of(slot * ENC, ENC), ENC)],
-                    send_sem=enc_send_sem.at[g],
-                    recv_sem=enc_recv_sem.at[slot],
-                    device_id=device(da, db),
-                    device_id_type=MESH,
-                )
-
-            when(reaches(da), send)
+    pl.semaphore_wait(barrier, jnp.where(inner, 8, 5))
+
+    @pl.when(inner)
+    def _():
+        for kind in (8, 7, 2):
+            enc_copy(kind).start()
+
+    for vertical in (0, 1):
+        onehot, geometry = enc_columns(vertical)
+        rows = slice(3 * vertical * ENC, 3 * (vertical + 1) * ENC)
+        enc_send[rows, :] = (dot(onehot, enc_table[...]) + geometry).astype(BF16)
+        for kind in ((4, 3) if vertical == 0 else (6, 5, 1)):
+            enc_copy(kind).start()
+    enc_recv[0:ENC, :] = enc_send[ENC : 2 * ENC, :]
 
     dec_rows[...] = jnp.zeros_like(dec_rows)
     dec_rows[0:1, 0 : 9 * DEC] = get_row(Arg.decode_sources)
@@ -301,28 +298,26 @@
         packet = dec_all if g == 0 else pltpu.roll(dec_all, dec_all.shape[1] - g * DEC, 1)
         meta_out[g] = packet[:, 0:128]
         meta_out[g, 2:3, :] = border
-        if g == 4:
-            meta_in[0] = meta_out[g]
-            continue
-        da, db = OFFSETS[g]
-
-        def meta_copy(da, db, g):
-            slot = slot_of(-da, -db) if da == 0 else jnp.where(
-                steps[1] == da, KINDS.index((1, -db)), KINDS.index((2, -db))
-            )
-            return pltpu.make_async_remote_copy(
-                src_ref=meta_out.at[g],
-                dst_ref=meta_in.at[slot],
-                send_sem=meta_send_sem.at[g],
-                recv_sem=meta_recv_sem.at[slot],
-                device_id=device(da, db),
-                device_id_type=MESH,
-            )
-
-        def send_meta(da=da, db=db, g=g):
-            meta_copy(da, db, g).start()
-
-        when(reaches(da), send_meta)
+    meta_in[0] = meta_out[4]
+
+    def meta_copy(kind):
+        da, db = place(kind)
+        return pltpu.make_async_remote_copy(
+            src_ref=meta_out.at[(da + 1) * 3 + db + 1],
+            dst_ref=meta_in.at[MIRROR[kind]],
+            send_sem=meta_send_sem.at[kind],
+            recv_sem=meta_recv_sem.at[MIRROR[kind]],
+            device_id=device(da, db),
+            device_id_type=MESH,
+        )
+
+    for kind in (3, 4, 5, 6, 1):
+        meta_copy(kind).start()
+
+    @pl.when(inner)
+    def _():
+        for kind in (7, 8, 2):
+            meta_copy(kind).start()
 
     corner_cols[...] = meta_out[4].T
     corner_rows = pl.ds(pl.multiple_of(jnp.where(even, 0, 2 * HALO), 2 * HALO), 2 * HALO)
@@ -512,34 +507,34 @@
         )
         comp[rows, :] = dot_last(far, border_onehot).astype(BF16)
 
-    for g in OTHERS:
-        da, db = OFFSETS[g]
-
-        def sent(da=da, db=db, g=g):
-            enc_copy(da, db, g).wait_send()
-            meta_copy(da, db, g).wait_send()
-
-        when(reaches(da), sent)
+    for kind in (1, 3, 4, 5, 6):
+        enc_copy(kind).wait_send()
+        meta_copy(kind).wait_send()
+
+    @pl.when(inner)
+    def _():
+        for kind in (2, 7, 8):
+            enc_copy(kind).wait_send()
+            meta_copy(kind).wait_send()
+
     relay(halo_mesh, mesh_recv_sem, mesh_copies[2])
     wait_for(halo_mesh, NODES, mesh_recv_sem, (1, 2, 5, 6, 7, 8))
-    for part in range(2, 4):
-        rows = slice(part * 256, (part + 1) * 256)
-        pre = base[rows, :] + dot(comp[(part - 2) * 256 : (part - 1) * 256, :], halo_mesh[NODES:, :])
-        msgs[rows, :] = norm_centred(dot(silu(pre).astype(BF16), get(Arg.process_output))).astype(BF16)
+    pre = base[HALF:, :] + dot(comp[...], halo_mesh[NODES:, :])
+    msgs[HALF:, :] = norm_centred(dot(silu(pre).astype(BF16), get(Arg.process_output))).astype(BF16)
     total = (near_total + dot(row_onehot(proc_target_row[:, HALF:], NODES), msgs[HALF:, :])).astype(BF16)
     hidden = silu(mesh_part[...] + dot(total, get(Arg.node_gather))).astype(BF16)
     mesh_new = (mesh_one[...].astype(F32) + norm_centred(dot(hidden, get(Arg.node_output)))).astype(BF16)
     mesh_out[...] = mesh_new
 
     halo_back[0:NODES, :] = dot(mesh_new, get(Arg.decode_source)).astype(BF16)
-    back_copies = spread(halo_back, back_send_sem, back_recv_sem)
+    back_copies = spread(halo_back, enc_send_sem, enc_recv_sem)
     dec_scatter = row_onehot(dec_targets[1:2, 0 : 9 * DEC], GRID)
     for kinds in ((0, 1), (3, 4), (2, 5, 6), (7, 8)):
         if 3 in kinds:
             sent_all(mesh_copies)
-            relay(halo_back, back_recv_sem, back_copies[2])
+            relay(halo_back, enc_recv_sem, back_copies[2])
         else:
-            wait_for(halo_back, NODES, back_recv_sem, [kind for kind in kinds if kind])
+            wait_for(halo_back, NODES, enc_recv_sem, [kind for kind in kinds if kind])
         hidden = []
         for kind in kinds:
             rows = slice(kind * DEC, (kind + 1) * DEC)
@@ -583,9 +578,10 @@
     dma = pltpu.SemaphoreType.DMA
     vmem = pltpu.VMEM
     scratch = [vmem(x.shape, x.dtype) for x in arrays]
-    scratch += [dma((35,))] + [dma((9,)) for _ in range(8)]
+    scratch += [dma((35,))] + [dma((9,)) for _ in range(6)]
     scratch += [
         vmem((24, 640), F32),
+        vmem((640, 24), F32),
         vmem((24, EDGES), F32),
         vmem((24, 896), F32),
         vmem((128, 24), F32),

time: 34.3 us -> 33.8 us (0.985)
  Pallas kernels: 33.6 us -> 33 us
    pallas_call x1, Pallas kernels: 32.8 us -> 32.3 us  [body(): pl.pallas_call(functools.partial(kernel, n_lat, n_lon), out_shape=(jax.Sh...]
where the time goes in v6:
time: 33.8 us; the launch traced here: 33.7 us
  Pallas kernels  33 us (98%)
  between operations  0.65 us (2%)
    pallas_call x1, Pallas kernels, body(): pl.pallas_call(functools.partial(kernel, n_lat, n_lon), out_shape=(jax.Sh...  32.3 us
    pallas_call x1, Pallas kernels, hand_over(): pl.pallas_call(hand_over_kernel, out_shape=tuple((jax.ShapeDtypeStruct(x....  0.74 us

profile of v6, /device:TPU:1, one launch (start us, length us, event | category | flops | bytes accessed | tf_op | source)
XLA Modules:
  0.0 33.7 jit_solution(1572284500824426832)
XLA Ops:
  0.6 32.3 %shard_map.338 = (bf16[256,512]{1,0:T(8,128)(2,1)S(1)}, bf16[64,512]{1,0:T(8,128)(2,1)S(1)}) custom-call(bf16[256,512]{1,0:T(8,128)(2,1)} %refs_0_.1, bf16[64,512]{1,0:T(8,128)(2,1)} %refs_1_.1, s32[576]{0:T(1024)} %refs_2_.1, s32[576]{0:T(1024)} %refs_3_.1, f32[4,576]{1,0:T(4,128)} %refs_4_.1, s32[2,2,32]{2,1,0:T(2,128)} %refs_5_.1, s32[1024]{0:T(1024)} %refs_6_.1, ...), custom_call_target="tpu_custom_call" | custom-call | flops 6000000000 | bytes 12000000 | tf_op jit(solution)/shard_map/pallas_call | solution.py:613
  32.9 0.7 %shard_map.339 = (bf16[256,512]{1,0:T(8,128)(2,1)}, bf16[64,512]{1,0:T(8,128)(2,1)}) custom-call(bf16[256,512]{1,0:T(8,128)(2,1)S(1)} %get-tuple-element.4.grid_ref, bf16[64,512]{1,0:T(8,128)(2,1)S(1)} %get-tuple-element.5.mesh_ref), custom_call_target="tpu_custom_call" | custom-call | tf_op jit(solution)/shard_map/pallas_call | solution.py:567

commit v7 on v6

--- a/solution.py
+++ b/solution.py
@@ -390,7 +390,12 @@
     enc_targets = by_kind(enc_rows[0:8, :], ENC)
     enc_tgt_onehot[...] = column_onehot(enc_targets.T[0 : 9 * ENC, 1:2], NODES)
     enc_scatter = row_onehot(enc_targets[1:2], NODES)
-    for name in (Arg.encode_output, Arg.mesh_output, Arg.process_output, Arg.node_output):
+    for name in (
+        Arg.encode_output,
+        Arg.mesh_output,
+        Arg.process_output,
+        Arg.node_output,
+    ):
         centre(name)
     for name in list(loads):
         get(name)
@@ -467,18 +472,6 @@
     near_total = dot(row_onehot(proc_target_row[:, 0:HALF], NODES), msgs[0:HALF, :])
 
     wait_for(meta_in, None, meta_recv_sem, range(1, 9))
-    dec_targets = by_kind(dec_rows[0:8, :], DEC)
-    dec_columns = dec_targets.T
-    dec_geometry = geometry_weights(get(Arg.decode_geometry))
-    for name in (Arg.decode_output, Arg.grid_output):
-        centre(name)
-    for kind in range(9):
-        rows = slice(kind * DEC, (kind + 1) * DEC)
-        columns = meta_in[kind].T[0:DEC]
-        dec_onehot[rows, :] = column_onehot(columns[:, 0:1], NODES)
-        dec_base[rows, :] = dot(
-            column_onehot(dec_columns[rows, 1:2], GRID), dec_table[...]
-        ) + dot(columns[:, 8:24].astype(BF16), dec_geometry)
     lane = lax.broadcasted_iota(jnp.int32, (8, 128), 1)
     tiles = []
     for tile in range(3):
@@ -528,6 +521,18 @@
 
     halo_back[0:NODES, :] = dot(mesh_new, get(Arg.decode_source)).astype(BF16)
     back_copies = spread(halo_back, enc_send_sem, enc_recv_sem)
+    for name in (Arg.decode_output, Arg.grid_output):
+        centre(name)
+    dec_targets = by_kind(dec_rows[0:8, :], DEC)
+    dec_columns = dec_targets.T
+    dec_geometry = geometry_weights(get(Arg.decode_geometry))
+    for kind in range(9):
+        rows = slice(kind * DEC, (kind + 1) * DEC)
+        columns = meta_in[kind].T[0:DEC]
+        dec_onehot[rows, :] = column_onehot(columns[:, 0:1], NODES)
+        dec_base[rows, :] = dot(
+            column_onehot(dec_columns[rows, 1:2], GRID), dec_table[...]
+        ) + dot(columns[:, 8:24].astype(BF16), dec_geometry)
     dec_scatter = row_onehot(dec_targets[1:2, 0 : 9 * DEC], GRID)
     for kinds in ((0, 1), (3, 4), (2, 5, 6), (7, 8)):
         if 3 in kinds:

time: 33.8 us -> 33.3 us (0.985)
  Pallas kernels: 33 us -> 32.4 us
    pallas_call x1, Pallas kernels: 32.3 us -> 31.7 us  [body(): pl.pallas_call(functools.partial(kernel, n_lat, n_lon), out_shape=(jax.Sh...]
where the time goes in v7:
time: 33.3 us; the launch traced here: 33.1 us
  Pallas kernels  32.4 us (97%)
  between operations  0.65 us (2%)
    pallas_call x1, Pallas kernels, body(): pl.pallas_call(functools.partial(kernel, n_lat, n_lon), out_shape=(jax.Sh...  31.7 us
    pallas_call x1, Pallas kernels, hand_over(): pl.pallas_call(hand_over_kernel, out_shape=tuple((jax.ShapeDtypeStruct(x....  0.74 us

profile of v7, /device:TPU:1, one launch (start us, length us, event | category | flops | bytes accessed | tf_op | source)
XLA Modules:
  0.0 33.1 jit_solution(2306461226430093831)
XLA Ops:
  0.6 31.7 %shard_map.338 = (bf16[256,512]{1,0:T(8,128)(2,1)S(1)}, bf16[64,512]{1,0:T(8,128)(2,1)S(1)}) custom-call(bf16[256,512]{1,0:T(8,128)(2,1)} %refs_0_.1, bf16[64,512]{1,0:T(8,128)(2,1)} %refs_1_.1, s32[576]{0:T(1024)} %refs_2_.1, s32[576]{0:T(1024)} %refs_3_.1, f32[4,576]{1,0:T(4,128)} %refs_4_.1, s32[2,2,32]{2,1,0:T(2,128)} %refs_5_.1, s32[1024]{0:T(1024)} %refs_6_.1, ...), custom_call_target="tpu_custom_call" | custom-call | flops 6000000000 | bytes 12000000 | tf_op jit(solution)/shard_map/pallas_call | solution.py:618
  32.3 0.7 %shard_map.339 = (bf16[256,512]{1,0:T(8,128)(2,1)}, bf16[64,512]{1,0:T(8,128)(2,1)}) custom-call(bf16[256,512]{1,0:T(8,128)(2,1)S(1)} %get-tuple-element.4.grid_ref, bf16[64,512]{1,0:T(8,128)(2,1)S(1)} %get-tuple-element.5.mesh_ref), custom_call_target="tpu_custom_call" | custom-call | tf_op jit(solution)/shard_map/pallas_call | solution.py:572

commit v8 on v7

--- a/solution.py
+++ b/solution.py
@@ -225,13 +225,17 @@
 
     load(FIRST)
     barrier = pltpu.get_barrier_semaphore()
-    for g in OTHERS:
-        da, db = OFFSETS[g]
-
-        def greet(da=da, db=db):
-            pl.semaphore_signal(barrier, inc=1, device_id=device(da, db), device_id_type=MESH)
-
-        when(reaches(da), greet)
+
+    def greet(kind):
+        pl.semaphore_signal(barrier, inc=1, device_id=device(*place(kind)), device_id_type=MESH)
+
+    @pl.when(inner)
+    def _():
+        for kind in (7, 8, 2):
+            greet(kind)
+
+    for kind in (5, 6, 3, 4, 1):
+        greet(kind)
     load(SECOND)
 
     @pl.when(jnp.logical_not(inner))

time: 33.3 us -> 33.2 us (level)
  no operation moved by 1% of the time
where the time goes in v8:
time: 33.2 us; the launch traced here: 33.1 us
  Pallas kernels  32.4 us (98%)
  between operations  0.65 us (2%)
    pallas_call x1, Pallas kernels, body(): pl.pallas_call(functools.partial(kernel, n_lat, n_lon), out_shape=(jax.Sh...  31.7 us
    pallas_call x1, Pallas kernels, hand_over(): pl.pallas_call(hand_over_kernel, out_shape=tuple((jax.ShapeDtypeStruct(x....  0.74 us

profile of v8, /device:TPU:1, one launch (start us, length us, event | category | flops | bytes accessed | tf_op | source)
XLA Modules:
  0.0 33.1 jit_solution(8187352079345237867)
XLA Ops:
  0.6 31.7 %shard_map.338 = (bf16[256,512]{1,0:T(8,128)(2,1)S(1)}, bf16[64,512]{1,0:T(8,128)(2,1)S(1)}) custom-call(bf16[256,512]{1,0:T(8,128)(2,1)} %refs_0_.1, bf16[64,512]{1,0:T(8,128)(2,1)} %refs_1_.1, s32[576]{0:T(1024)} %refs_2_.1, s32[576]{0:T(1024)} %refs_3_.1, f32[4,576]{1,0:T(4,128)} %refs_4_.1, s32[2,2,32]{2,1,0:T(2,128)} %refs_5_.1, s32[1024]{0:T(1024)} %refs_6_.1, ...), custom_call_target="tpu_custom_call" | custom-call | flops 6000000000 | bytes 12000000 | tf_op jit(solution)/shard_map/pallas_call | solution.py:622
  32.3 0.7 %shard_map.339 = (bf16[256,512]{1,0:T(8,128)(2,1)}, bf16[64,512]{1,0:T(8,128)(2,1)}) custom-call(bf16[256,512]{1,0:T(8,128)(2,1)S(1)} %get-tuple-element.4.grid_ref, bf16[64,512]{1,0:T(8,128)(2,1)S(1)} %get-tuple-element.5.mesh_ref), custom_call_target="tpu_custom_call" | custom-call | tf_op jit(solution)/shard_map/pallas_call | solution.py:576
